TPU v7x, 256 devices: a whole 4x4x8 slice. The times are simulated.
256 devices in a mesh: modes: 4 (over x), elem: 64 (over y, z, core).
Axes of the slice: x: 4, y: 4, z: 8, core: 2. Of those that a mesh axis runs over, the one named last changes fastest.
Arguments:
- velocity: float32 [3, 256, 10, 10, 512], P(None, 'elem', None, None, 'modes'), may hold values from -0.3 to 0.3
- element_slot: int32 [64, 4], P('elem'), may hold values from 0 to 3, each once within a row
- lid_noslip: int32 [256], P('modes'), may hold values 0 or 1
Outputs:
- new_velocity: float32 [3, 256, 10, 10, 512], P(None, 'elem', None, None, 'modes')
Inputs may be any that keep to these rules, and one draw needn't show every extreme that they name: `element_slot`: each row orders the 4 slots of one index block, each slot once.
All inputs are finite; a program needn't handle non-finite values. No bound on the sum of `lid_noslip` on one device may be relied on, other than what follows from the above.
Results may differ from a plain program's by a relative error of at most 0.0003.
Values sent between devices are 32-bit elements; how exact they have to be, the bound alone decides.
A program may use at most 128 MiB of HBM per device.

v0:
```python
import math

import jax
import jax.numpy as jnp
import numpy as np
from jax import lax
from jax.sharding import PartitionSpec as P

P_SIZE = 10
M = 256
Q = 768
ER = 4
EZ_DEV = 1
E_DEV = 4
ITERS = 3


LAMBDA_COEF = 20.0
INV_NU = 10.0
R_INNER = 1.0
SWIRL_SLOPE = -1.0 / 3.0
SWIRL_CURVE = 4.0 / 3.0
highest = lax.Precision.HIGHEST


def extended(block, sides, width):
    for axis, dim in sides:
        count = lax.axis_size(axis)
        forward = [(i, i + 1) for i in range(count - 1)]
        backward = [(target, source) for source, target in forward]
        low = lax.ppermute(
            lax.slice_in_dim(block, block.shape[dim] - width, None, axis=dim), axis, forward
        )
        high = lax.ppermute(lax.slice_in_dim(block, 0, width, axis=dim), axis, backward)
        block = jnp.concatenate([low, block, high], axis=dim)
    return block


def legendre_rows(abscissa, degree):
    table_rows = [abscissa * 0.0 + 1.0, abscissa.copy()]
    for degree_now in range(2, degree + 1):
        table_rows.append(
            ((2 * degree_now - 1) * abscissa * table_rows[-1] - (degree_now - 1) * table_rows[-2])
            / degree_now
        )
    return table_rows


def gll_tables(points):
    degree = points - 1
    abscissa = -np.cos(np.pi * np.arange(points) / degree)
    for _ in range(60):
        legendre = legendre_rows(abscissa, degree)
        abscissa = abscissa - (abscissa * legendre[degree] - legendre[degree - 1]) / (
            points * legendre[degree]
        )
    legendre = legendre_rows(abscissa, degree)
    last_row = legendre[degree]
    weights = 2.0 / (degree * points * last_row**2)
    identity = np.eye(points)
    distance = abscissa[:, None] - abscissa[None, :] + identity
    derivative = last_row[:, None] / (last_row[None, :] * distance) * (1.0 - identity)
    derivative[0, 0] = -degree * points / 4.0
    derivative[degree, degree] = degree * points / 4.0
    return (
        jnp.asarray(abscissa, jnp.float32),
        jnp.asarray(weights, jnp.float32),
        jnp.asarray(derivative, jnp.float32),
    )


def radial_nodes(abscissa, column_ids):
    return R_INNER + (column_ids[:, None] + 0.5 * (abscissa[None, :] + 1.0)) / ER


def fourier_tables(mode_count, planes):
    mode_ids = jnp.arange(mode_count, dtype=jnp.int32)
    plane_ids = jnp.arange(planes, dtype=jnp.int32)
    phase_ids = mode_ids[:, None] * plane_ids[None, :] % planes
    angles = phase_ids.astype(jnp.float32) * (2.0 * math.pi / planes)
    cosine = jnp.cos(angles)
    sine_part = jnp.sin(angles)
    weight = jnp.where(mode_ids == 0, 1.0, 2.0).astype(jnp.float32)[:, None]
    inverse_table = jnp.stack([weight * cosine, -weight * sine_part], axis=1).reshape(
        2 * mode_count, planes
    )
    forward_table = (
        jnp.stack([cosine, -sine_part], axis=1).reshape(2 * mode_count, planes) / planes
    ).T
    return (inverse_table, forward_table)


def times_unit(values):
    pair_view = values.reshape(values.shape[:-1] + (values.shape[-1] // 2, 2))
    return jnp.stack([-pair_view[..., 1], pair_view[..., 0]], axis=-1).reshape(values.shape)


def curl_modes(velocity_hat, derivative, inv_radius, wave_number):
    radial_u, swirl_u, axial_u = (velocity_hat[0], velocity_hat[1], velocity_hat[2])
    metric_scale = 2.0 * ER

    def along_r(field_data):
        return (
            jnp.einsum("ia,...ajc->...ijc", derivative, field_data, precision=highest)
            * metric_scale
        )

    def along_z(field_data):
        return (
            jnp.einsum("jb,...ibc->...ijc", derivative, field_data, precision=highest)
            * metric_scale
        )

    def beside_all(field_data):
        return wave_number * times_unit(field_data)

    curl_r = beside_all(axial_u) * inv_radius - along_z(swirl_u)
    curl_t = along_z(radial_u) - along_r(axial_u)
    curl_z = along_r(swirl_u) + swirl_u * inv_radius - beside_all(radial_u) * inv_radius
    return jnp.stack([curl_r, curl_t, curl_z])


def plane_products(velocity_hat, curl_hat, radius, inverse_table, forward_table):
    dims_in = velocity_hat.shape
    row_count = math.prod(dims_in[1:-1])
    stacked = jnp.concatenate([velocity_hat, curl_hat]).reshape(6 * row_count, dims_in[-1])
    planes = jnp.dot(stacked, inverse_table, precision=highest).reshape(6, row_count, -1)
    radius_rows = jnp.broadcast_to(radius, dims_in[1:-1]).reshape(row_count, 1)
    swirl_base = SWIRL_SLOPE * radius_rows + SWIRL_CURVE / radius_rows
    spin_base = 2.0 * SWIRL_SLOPE
    radial_u, swirl_u, axial_u = (planes[0], planes[1], planes[2])
    curl_r, curl_t, curl_z = (planes[3], planes[4], planes[5])
    push_r = swirl_u * curl_z - axial_u * curl_t + spin_base * swirl_u + swirl_base * curl_z
    push_t = axial_u * curl_r - radial_u * curl_z - spin_base * radial_u
    push_z = radial_u * curl_t - swirl_u * curl_r - swirl_base * curl_r
    pushed = jnp.stack([push_r, push_t, push_z]).reshape(3 * row_count, -1)
    return jnp.dot(pushed, forward_table, precision=highest).reshape(dims_in)


def to_helical(field_data):
    turned = times_unit(field_data[1])
    return jnp.stack([field_data[0] + turned, field_data[0] - turned, field_data[2]])


def from_helical(field_data):
    radial_u = (field_data[0] + field_data[1]) * 0.5
    swirl_u = times_unit(field_data[1] - field_data[0]) * 0.5
    return jnp.stack([radial_u, swirl_u, field_data[2]])


def helmholtz_parts(abscissa, weights, derivative, wave_cols):
    radius = radial_nodes(abscissa, jnp.arange(ER).astype(jnp.float32))
    outer_w = weights[:, None] * weights[None, :]
    weighted_r = outer_w[None] * radius[:, :, None]
    quarter_h = 0.25 / (ER * ER)
    mass_r = outer_w[None] * quarter_h * radius[:, :, None]
    mass_over_r = outer_w[None] * quarter_h / radius[:, :, None]
    offsets = jnp.array([1.0, -1.0, 0.0], dtype=jnp.float32)
    wave_number = wave_cols[None, :] + offsets[:, None]
    mode_mass = (
        mass_over_r[None, :, :, :, None] * (wave_number * wave_number)[:, None, None, None, :]
        + LAMBDA_COEF * mass_r[None, :, :, :, None]
    )
    deriv_square = derivative * derivative
    stiff_diag = jnp.einsum(
        "qi,eqj->eij", deriv_square, weighted_r, precision=highest
    ) + jnp.einsum("qj,eiq->eij", deriv_square, weighted_r, precision=highest)
    return (weighted_r, mode_mass[:, None], stiff_diag)


def apply_local(field_data, derivative, weighted_r, mode_mass):
    grad_i = jnp.einsum("ia,szeajc->szeijc", derivative, field_data, precision=highest)
    grad_j = jnp.einsum("jb,szeibc->szeijc", derivative, field_data, precision=highest)
    flux_weight = weighted_r[None, None, :, :, :, None]
    stiff_part = jnp.einsum(
        "ia,szeijc->szeajc", derivative, flux_weight * grad_i, precision=highest
    ) + jnp.einsum("jb,szeijc->szeibc", derivative, flux_weight * grad_j, precision=highest)
    return stiff_part + mode_mass * field_data


def sum_columns(field_data):
    shared = field_data[..., :, :-1, -1, :, :] + field_data[..., :, 1:, 0, :, :]
    field_data = field_data.at[..., :, :-1, -1, :, :].set(shared)
    return field_data.at[..., :, 1:, 0, :, :].set(shared)


def sum_rows(field_data):
    shared = field_data[..., :-1, :, :, -1, :] + field_data[..., 1:, :, :, 0, :]
    field_data = field_data.at[..., :-1, :, :, -1, :].set(shared)
    return field_data.at[..., 1:, :, :, 0, :].set(shared)


def assemble(field_data):
    field_data = sum_rows(sum_columns(field_data))
    low_face = field_data[..., 0, :, :, 0, :]
    high_face = field_data[..., -1, :, :, -1, :]
    face_pairs = jnp.stack([low_face, high_face])
    around_faces = extended(face_pairs, (("elem", 0),), 1)
    field_data = field_data.at[..., 0, :, :, 0, :].set(low_face + around_faces[0])
    return field_data.at[..., -1, :, :, -1, :].set(high_face + around_faces[3])


def keep_mask(z_ids, total_rows, noslip_cols):
    node_ids = jnp.arange(P_SIZE, dtype=jnp.int32)[None, :]
    column_grid = jnp.arange(ER, dtype=jnp.int32)[:, None]
    wall_nodes = (column_grid == 0) & (node_ids == 0) | (column_grid == ER - 1) & (
        node_ids == P_SIZE - 1
    )
    wall_keep = 1.0 - wall_nodes.astype(jnp.float32)
    row_grid = z_ids[:, None]
    lid_nodes = (
        (row_grid == 0) & (node_ids == 0) | (row_grid == total_rows - 1) & (node_ids == P_SIZE - 1)
    ).astype(jnp.float32)
    lid_comp = jnp.stack([noslip_cols, noslip_cols, jnp.ones_like(noslip_cols)])
    return wall_keep[None, None, :, :, None, None] * (
        1.0 - lid_nodes[None, :, None, None, :, None] * lid_comp[:, None, None, None, None, :]
    )


def inverse_multiplicity(z_ids, total_rows):
    node_ids = jnp.arange(P_SIZE, dtype=jnp.int32)[None, :]
    column_grid = jnp.arange(ER, dtype=jnp.int32)[:, None]
    share_col = (
        (node_ids == 0) & (column_grid > 0) | (node_ids == P_SIZE - 1) & (column_grid < ER - 1)
    ).astype(jnp.float32)
    row_grid = z_ids[:, None]
    share_row = (
        (node_ids == 0) & (row_grid > 0) | (node_ids == P_SIZE - 1) & (row_grid < total_rows - 1)
    ).astype(jnp.float32)
    counted = (1.0 + share_col)[None, :, :, None] * (1.0 + share_row)[:, None, None, :]
    return (1.0 / counted)[None, :, :, :, :, None]


def mode_inner(left_vec, right_vec, inv_mult):
    local_sum = jnp.sum(left_vec * right_vec * inv_mult, axis=(1, 2, 3, 4))
    return local_sum.reshape(3, -1, 2).sum(-1)


def spread(coefficients):
    return jnp.repeat(coefficients, 2, axis=-1).reshape(3, 1, 1, 1, 1, -1)


def global_inner(left_vec, right_vec, inv_mult):
    return lax.psum(mode_inner(left_vec, right_vec, inv_mult), "elem")


def on_device(velocity, element_slot, lid_noslip):
    abscissa, weights, derivative = gll_tables(P_SIZE)
    modes_count = lax.axis_size("modes")
    elem_count = lax.axis_size("elem")
    mode_index = lax.axis_index("modes")
    elem_index = lax.axis_index("elem")
    columns = velocity.shape[-1]
    sub_count = E_DEV // modes_count
    slot_of = element_slot[0]
    onehot = (slot_of[:, None] == jnp.arange(E_DEV, dtype=jnp.int32)[None, :]).astype(jnp.float32)
    grid_vel = jnp.einsum("gs,tsijc->tgijc", onehot, velocity, precision=highest)
    wave_local = ((mode_index * columns + jnp.arange(columns, dtype=jnp.int32)) // 2).astype(
        jnp.float32
    )
    radius_all = radial_nodes(
        abscissa, (jnp.arange(E_DEV, dtype=jnp.int32) % ER).astype(jnp.float32)
    )
    group_radius = lax.dynamic_slice_in_dim(radius_all, mode_index * sub_count, sub_count, 0)
    inverse_table, forward_table = fourier_tables(M, Q)
    split_vel = grid_vel.reshape(3, modes_count, sub_count, P_SIZE, P_SIZE, columns)
    curl_hat = curl_modes(grid_vel, derivative, (1.0 / radius_all)[:, :, None, None], wave_local)
    split_curl = curl_hat.reshape(3, modes_count, sub_count, P_SIZE, P_SIZE, columns)
    planes_vel, planes_curl = (
        lax.all_to_all(split_vel, "modes", split_axis=1, concat_axis=5, tiled=True),
        lax.all_to_all(split_curl, "modes", split_axis=1, concat_axis=5, tiled=True),
    )
    pushed_hat = plane_products(
        planes_vel, planes_curl, group_radius[:, :, None], inverse_table, forward_table
    )
    returned = lax.all_to_all(pushed_hat, "modes", split_axis=5, concat_axis=1, tiled=True)
    nonlinear = returned.reshape(3, EZ_DEV, ER, P_SIZE, P_SIZE, columns)
    grid_six = grid_vel.reshape(3, EZ_DEV, ER, P_SIZE, P_SIZE, columns)
    forcing = LAMBDA_COEF * grid_six + INV_NU * nonlinear
    radius = radial_nodes(abscissa, jnp.arange(ER).astype(jnp.float32))
    outer_w = weights[:, None] * weights[None, :]
    mass_r = outer_w[None] * (0.25 / (ER * ER)) * radius[:, :, None]
    loads = mass_r[None, None, :, :, :, None] * to_helical(forcing)
    weighted_r, mode_mass, stiff_diag = helmholtz_parts(abscissa, weights, derivative, wave_local)
    total_rows = EZ_DEV * elem_count
    z_ids = elem_index * EZ_DEV + jnp.arange(EZ_DEV, dtype=jnp.int32)
    noslip_cols = jnp.repeat(lid_noslip.astype(jnp.float32), 2)
    keep_nodes = keep_mask(z_ids, total_rows, noslip_cols)
    inv_mult = inverse_multiplicity(z_ids, total_rows)
    diag_local = jnp.broadcast_to(stiff_diag[None, None, :, :, :, None] + mode_mass, loads.shape)
    both_sums = assemble(jnp.stack([loads, diag_local]))
    residual = keep_nodes * both_sums[0]
    jacobi_inv = keep_nodes / both_sums[1]
    solution = jnp.zeros_like(residual)
    precond = jacobi_inv * residual
    direction = precond
    precond_dot = global_inner(residual, precond, inv_mult)
    for turn_index in range(ITERS):
        image_vec = keep_nodes * assemble(apply_local(direction, derivative, weighted_r, mode_mass))
        step_length = precond_dot / global_inner(direction, image_vec, inv_mult)
        solution = solution + spread(step_length) * direction
        if turn_index + 1 < ITERS:
            residual = residual - spread(step_length) * image_vec
            precond = jacobi_inv * residual
            next_dot = global_inner(residual, precond, inv_mult)
            direction = precond + spread(next_dot / precond_dot) * direction
            precond_dot = next_dot
    result_grid = from_helical(solution).reshape(3, E_DEV, P_SIZE, P_SIZE, columns)
    return jnp.einsum("gs,tgijc->tsijc", onehot, result_grid, precision=highest)


def solution(mesh):
    in_specs = (P(None, "elem", None, None, "modes"), P("elem", None), P("modes"))
    out_specs = P(None, "elem", None, None, "modes")
    return jax.shard_map(
        on_device, mesh=mesh, in_specs=in_specs, out_specs=out_specs, check_vma=False
    )
```

profile of v0, /device:TPU:1, one launch (start us, length us, event | category | flops | bytes accessed | tf_op | source)
XLA Modules:
  0.0 991.3 jit_solution(2241935176612515606)
XLA Ops:
  1.1 1.5 fusion.86
  3.6 2.3 copy.644
  5.9 5.3 slice_negate_fusion.2
  11.2 4.5 pad_maximum_fusion
  15.7 2.5 copy.645
  18.2 2.3 copy.657
  20.5 5.3 slice_negate_fusion.1
  26.3 4.5 pad_maximum_fusion.1
  30.8 2.5 copy.658
  36.7 4.8 all-to-all-start.1
  41.6 4.4 fusion.35
  46.1 3.8 broadcast_multiply_fusion
  49.9 3.8 fusion.37
  54.7 1.5 pad_maximum_fusion.4
  56.2 2.7 maximum_multiply_fusion
  62.0 1.5 copy.642
  64.0 4.4 all-to-all-start
  68.5 2.4 copy.663
  70.8 3.3 reshape.1743
  74.2 2.4 copy.664
  76.6 3.2 reshape.1764
  83.5 3.4 maximum_reduce_fusion
  88.1 5.0 fusion.100
  95.3 1.8 stack.83
  98.0 4.7 fusion.7
  102.6 14.9 %copy.665 = f32[3,1,1,10,10,512]{4,2,3,1,0,5:T(1,128)} copy(f32[3,1,1,10,10,512]{5,4,3,0,2,1:T(8,128)} %fusion.7) | data formatting | bytes 1228800 | tf_op jit(solution)/shard_map/dot_general | solution.py:137
  118.0 72.3 %reduce.58 = f32[512,3,10,10]{3,2,1,0:T(8,128)} reduce(f32[512,3,1,10,1,10]{5,4,3,2,1,0:T(1,128)} %bitcast.333, f32[]{:T(128)} %broadcast.1232), dimensions={2,4}, to_apply=%bitcast.288.reduce_sub_computation | reduce | bytes 1228804
  190.3 8.0 reshape.1777
  198.3 4.2 all-to-all-start.2
  203.9 6.1 all-to-all-done.2
  210.0 2.4 reduce.59
  212.4 17.0 %reshape.1778 = f32[512,3,1,10,1,10]{5,4,3,2,1,0:T(1,128)} reshape(f32[4,38400]{1,0:T(4,128)S(1)} %reduce.59) | data formatting | bytes 1228800
  229.4 14.2 %copy.666 = f32[3,1,1,10,10,512]{5,2,4,3,1,0:T(1,128)S(1)} copy(f32[3,1,1,10,10,512]{4,2,3,1,0,5:T(1,128)} %bitcast.332) | data formatting | bytes 1228800 | tf_op jit(solution)/shard_map/all_to_all | solution.py:276
  245.1 2.9 slice_negate_fusion
  248.0 3.0 pad_maximum_fusion.2
  255.0 1.9 fusion.69
  256.9 1.6 scatter.54
  258.9 7.4 collective-permute-start
  267.9 2.1 collective-permute-start.1
  270.1 4.0 collective-permute-done.1
  281.3 1.8 dynamic-slice_select_fusion.2
  285.5 1.9 collective-permute-start.2
  289.8 2.9 collective-permute-start.3
  293.4 2.6 collective-permute-done.3
  298.4 125.2 %all-reduce = (f32[3,64]{1,0:T(4,128)S(1)}, f32[3,64]{1,0:T(4,128)S(1)}) all-reduce(f32[3,64]{1,0:T(4,128)S(1)} %reduce_sum.109, f32[3,64]{1,0:T(4,128)S(1)} %reduce_sum.111), channel_id=1, replica_groups=mesh['modes'=4,'elem'=64] {'elem'}, use_global_device_ids=true, to_apply=%region_4.5 | all-reduce | flops 384 | bytes 3072 | tf_op jit(solution)/shard_map/psum | solution.py:244
  425.9 128.5 %psum.44 = f32[3,64]{1,0:T(4,128)S(1)} all-reduce(f32[3,64]{1,0:T(4,128)S(1)} %reduce_sum.113), channel_id=1, replica_groups=mesh['modes'=4,'elem'=64] {'elem'}, use_global_device_ids=true, to_apply=%region_12.13 | all-reduce | flops 192 | bytes 1536 | tf_op jit(solution)/shard_map/psum | solution.py:244
  560.7 2.4 dynamic-slice_select_fusion.1
  563.1 2.8 scatter.66
  565.9 1.6 scatter.69
  568.3 1.9 collective-permute-start.4
  571.5 2.2 collective-permute-start.5
  573.7 3.9 collective-permute-done.5
  577.7 2.2 fusion.73
  582.8 120.7 %psum.45 = f32[3,64]{1,0:T(4,128)S(1)} all-reduce(f32[3,64]{1,0:T(4,128)S(1)} %reduce_sum.115), channel_id=1, replica_groups=mesh['modes'=4,'elem'=64] {'elem'}, use_global_device_ids=true, to_apply=%region_15.16 | all-reduce | flops 192 | bytes 1536 | tf_op jit(solution)/shard_map/psum | solution.py:244
  707.3 127.4 %psum.46 = f32[3,64]{1,0:T(4,128)S(1)} all-reduce(f32[3,64]{1,0:T(4,128)S(1)} %reduce_sum.117), channel_id=1, replica_groups=mesh['modes'=4,'elem'=64] {'elem'}, use_global_device_ids=true, to_apply=%region_18.19 | all-reduce | flops 192 | bytes 1536 | tf_op jit(solution)/shard_map/psum | solution.py:244
  840.1 1.8 dynamic-slice_select_fusion
  843.6 1.9 collective-permute-start.6
  845.7 2.4 collective-permute-start.7
  848.1 3.1 collective-permute-done.7
  853.1 121.5 %psum.47 = f32[3,64]{1,0:T(4,128)S(1)} all-reduce(f32[3,64]{1,0:T(4,128)S(1)} %reduce_sum.119), channel_id=1, replica_groups=mesh['modes'=4,'elem'=64] {'elem'}, use_global_device_ids=true, to_apply=%region_21.22 | all-reduce | flops 192 | bytes 1536 | tf_op jit(solution)/shard_map/psum | solution.py:244
  976.7 4.5 fusion.97
  981.2 3.4 copy.754
  985.6 1.5 copy.728
  988.5 2.6 convolution_bitcast_fusion.6
  (212 shorter events, 73.4 us)
Async XLA Ops:
  0.0 1.1 copy-start
  1.1 1.6 copy-start.15
  30.8 2.5 copy-start.20
  36.7 27.3 %all-to-all-start.1 = ((f32[3,4,1,10,10,128]{5,2,4,3,0,1:T(1,128)}), f32[3,4,1,10,10,128]{5,2,4,3,0,1:T(1,128)S(1)}, u32[]{:S(2)}, u32[]{:S(2)}) async-start(f32[3,4,1,10,10,128]{5,2,4,3,0,1:T(1,128)} %copy.661), calls=%async_computation.1 | async-start | bytes 1228800 | tf_op jit(solution)/shard_map/all_to_all | solution.py:271
  41.6 12.1 %copy-start.17 = (f32[10]{0:T(128)S(1)}, f32[10]{0:T(128)}, u32[]{:S(2)}) copy-start(f32[10]{0:T(128)} %constant.488.clone) | copy-start | bytes 124
  41.6 12.9 %copy-start.21 = (s32[64]{0:T(128)S(1)}, s32[64]{0:T(128)}, u32[]{:S(2)}) copy-start(s32[64]{0:T(128)} %param.41) | copy-start | bytes 772
  56.2 2.7 copy-start.25
  56.2 4.6 copy-start.24
  56.2 5.5 copy-start.16
  64.0 16.8 %copy-start.13 = (f32[4,10,10]{2,1,0:T(8,128)}, f32[4,10,10]{2,1,0:T(8,128)S(1)}, u32[]{:S(2)}) copy-start(f32[4,10,10]{2,1,0:T(8,128)S(1)} %get-tuple-element.244) | copy-start | bytes 4804
  64.0 16.9 %copy-start.11 = (f32[4,10,10]{2,1,0:T(8,128)}, f32[4,10,10]{2,1,0:T(8,128)S(1)}, u32[]{:S(2)}) copy-start(f32[4,10,10]{2,1,0:T(8,128)S(1)} %get-tuple-element.243) | copy-start | bytes 4804
  64.0 18.2 %all-to-all-start = ((f32[3,4,1,10,10,128]{5,2,4,3,0,1:T(1,128)}), f32[3,4,1,10,10,128]{5,2,4,3,0,1:T(1,128)}, u32[]{:S(2)}, u32[]{:S(2)}) async-start(f32[3,4,1,10,10,128]{5,2,4,3,0,1:T(1,128)} %copy.642), calls=%async_computation | async-start | bytes 1228800 | tf_op jit(solution)/shard_map/all_to_all | solution.py:270
  70.8 3.4 copy-start.2
  82.2 1.3 copy-start.9
  94.2 3.8 copy-start.3
  190.3 12.2 %copy-start.19 = (f32[3]{0:T(128)S(1)}, f32[3]{0:T(128)}, u32[]{:S(2)}) copy-start(f32[3]{0:T(128)} %constant.490.clone) | copy-start | bytes 40
  198.3 11.7 %all-to-all-start.2 = ((f32[4,1,38400]{2,1,0:T(1,128)}), f32[4,1,38400]{2,1,0:T(1,128)S(1)}, u32[]{:S(2)}, u32[]{:S(2)}) async-start(f32[4,1,38400]{2,1,0:T(1,128)} %reshape.1777), calls=%async_computation.2 | async-start | bytes 1228800 | tf_op jit(solution)/shard_map/all_to_all | solution.py:276
  252.5 2.2 copy-start.6
  255.0 11.4 %copy-start.14 = (f32[4,10,10]{2,1,0:T(8,128)S(1)}, f32[4,10,10]{2,1,0:T(8,128)}, u32[]{:S(2)}) copy-start(f32[4,10,10]{2,1,0:T(8,128)} %copy-done.13) | copy-start | bytes 4804
  255.0 11.6 %copy-start.12 = (f32[4,10,10]{2,1,0:T(8,128)S(1)}, f32[4,10,10]{2,1,0:T(8,128)}, u32[]{:S(2)}) copy-start(f32[4,10,10]{2,1,0:T(8,128)} %copy-done.11) | copy-start | bytes 4804
  255.0 12.1 %copy-start.23 = (s32[6]{0:T(128)S(1)}, s32[6]{0:T(128)}, u32[]{:S(2)}) copy-start(s32[6]{0:T(128)} %constant.485.clone.1) | copy-start | bytes 76
  258.9 11.1 %collective-permute-start = (f32[1,2,3,4,10,128]{5,3,4,2,1,0:T(4,128)S(1)}, f32[1,2,3,4,10,128]{5,3,4,2,1,0:T(4,128)S(1)}, u32[]{:S(2)}, u32[]{:S(2)}) collective-permute-start(f32[1,2,3,4,10,128]{5,3,4,2,1,0:T(4,128)S(1)} %get-tuple-element.223), channel_id=1, source_target_pairs={{0,1},{1,2},{2,3},{3,4},{4,5},{5,6},{6,7},{7,8},{8,9},{9,10},{10,1... | collective-permute-start | bytes 368648 | tf_op jit(solution)/shard_map/ppermute | solution.py:31
  267.9 6.2 collective-permute-start.1
  275.5 0.7 copy-start.10
  275.7 4.5 copy-start.5
  281.3 11.4 %copy-start.22 = (s32[6]{0:T(128)S(1)}, s32[6]{0:T(128)}, u32[]{:S(2)}) copy-start(s32[6]{0:T(128)} %constant.486.clone.1) | copy-start | bytes 76
  285.5 3.5 collective-permute-start.2
  289.8 6.2 collective-permute-start.3
  559.9 0.8 copy-start.8
  568.3 3.2 collective-permute-start.4
  571.5 6.2 collective-permute-start.5
  579.8 0.8 copy-start.4
  843.6 4.5 collective-permute-start.6
  845.7 5.5 collective-permute-start.7
  981.2 3.4 copy-start.7
  987.1 1.5 copy-start.18
  987.1 4.1 copy-start.1
where the time goes:
time: 1000 us; the launch traced here: 991 us
  blocking collectives  623 us (62%)
  other arithmetic  156 us (16%)
  local copies, waits for them, and re-layouts  126 us (13%)
  starting transfers between devices  36.3 us (4%)
  matrix products  28.1 us (3%)
  waiting for transfers between devices  20.1 us (2%)
    psum x5, blocking collectives, global_inner(): return lax.psum(mode_inner(left_vec, right_vec, inv_mult), 'elem')  623 us
    unnamed x1, other arithmetic  72.3 us
    unnamed x60, local copies, waits for them, and re-layouts  33.2 us
  transfers between devices with their start and end apart: 11, of which 7 were waited for; matrix products, arithmetic and copies ran while one was open for 4% of the time, Pallas kernels for 0%

commit v1 on v0

v1 whole, which is shorter than its diff:
```python
import functools

import jax
import jax.numpy as jnp
import ml_dtypes
import numpy as np
from jax import lax
from jax.experimental import pallas as pl
from jax.experimental.pallas import tpu as pltpu
from jax.sharding import PartitionSpec as P

PS = 10
NODES = PS * PS
R = 112
M = 256
Q = 768
ER = 4
LANES = 128
LAMBDA_COEF = 20.0
INV_NU = 10.0
R_INNER = 1.0
SWIRL_SLOPE = -1.0 / 3.0
SWIRL_CURVE = 4.0 / 3.0
MESH = pl.DeviceIdType.MESH
F32 = jnp.float32
BF16 = jnp.bfloat16


def legendre_rows(abscissa, degree):
    table_rows = [abscissa * 0.0 + 1.0, abscissa.copy()]
    for degree_now in range(2, degree + 1):
        table_rows.append(
            ((2 * degree_now - 1) * abscissa * table_rows[-1] - (degree_now - 1) * table_rows[-2])
            / degree_now
        )
    return table_rows


def gll_tables(points):
    degree = points - 1
    abscissa = -np.cos(np.pi * np.arange(points) / degree)
    for _ in range(60):
        legendre = legendre_rows(abscissa, degree)
        abscissa = abscissa - (abscissa * legendre[degree] - legendre[degree - 1]) / (
            points * legendre[degree]
        )
    legendre = legendre_rows(abscissa, degree)
    last_row = legendre[degree]
    weights = 2.0 / (degree * points * last_row**2)
    identity = np.eye(points)
    distance = abscissa[:, None] - abscissa[None, :] + identity
    derivative = last_row[:, None] / (last_row[None, :] * distance) * (1.0 - identity)
    derivative[0, 0] = -degree * points / 4.0
    derivative[degree, degree] = degree * points / 4.0
    return abscissa, weights, derivative


def halves(values):
    high = values.astype(ml_dtypes.bfloat16)
    low = (values - high.astype(np.float64)).astype(ml_dtypes.bfloat16)
    return high, low


@functools.cache
def constants():
    xi, w, deriv = gll_tables(PS)
    eye = np.eye(PS)
    radius = R_INNER + (np.arange(ER)[:, None] + 0.5 * (xi[None, :] + 1.0)) / ER
    ww = np.outer(w, w)

    def operator(rows):
        padded = np.zeros((R, LANES))
        padded[:NODES, :NODES] = rows
        high, low = halves(padded)
        return np.concatenate([high, high, low], axis=1)

    slope_r = operator(2.0 * ER * np.kron(deriv, eye))
    slope_z = operator(2.0 * ER * np.kron(eye, deriv))
    slopes = np.concatenate([slope_r, slope_z], axis=0)

    stiff, stiff_diag = [], np.zeros((ER, PS, PS))
    for ir in range(ER):
        along_i = deriv.T @ np.diag(w * radius[ir]) @ deriv
        along_j = deriv.T @ np.diag(w) @ deriv
        whole = np.kron(along_i, np.diag(w)) + np.kron(np.diag(w * radius[ir]), along_j)
        stiff_diag[ir] = np.diag(whole).reshape(PS, PS)
        stiff.append(operator(whole - np.diag(np.diag(whole))))
    stiff = np.stack(stiff)

    quarter_h = 0.25 / (ER * ER)
    mass_r = ww[None] * quarter_h * radius[:, :, None]
    mass_over_r = ww[None] * quarter_h / radius[:, :, None]

    def radial_sum(values):
        total = values.copy()
        total[:-1, -1] += values[1:, 0]
        total[1:, 0] += values[:-1, -1]
        return total

    diag_fixed = radial_sum(stiff_diag + LAMBDA_COEF * mass_r)
    diag_square = radial_sum(mass_over_r)
    diag_fixed[0, 0] = 0.0
    diag_fixed[-1, -1] = 0.0

    geometry = np.zeros((3 * ER + 2, R, LANES))
    geometry[0:ER, :NODES] = mass_r.reshape(ER, NODES, 1)
    geometry[ER : 2 * ER, :NODES] = diag_fixed.reshape(ER, NODES, 1)
    geometry[2 * ER : 3 * ER, :NODES] = diag_square.reshape(ER, NODES, 1)
    geometry[3 * ER] = 1.0
    geometry[3 * ER, :NODES] = (R_INNER + 0.5 * (np.repeat(xi, PS) + 1.0) / ER)[:, None]
    face = np.zeros((PS, PS))
    face[:, 0] = 1.0
    face[:, -1] = 2.0
    geometry[3 * ER + 1, :NODES] = face.reshape(NODES, 1)

    modes = np.arange(M)
    angles = (modes[:, None] * np.arange(Q)[None, :] % Q) * (2.0 * np.pi / Q)
    weight = np.where(modes == 0, 1.0, 2.0)[:, None]
    inverse = np.stack([weight * np.cos(angles), -weight * np.sin(angles)], axis=1)
    inverse = inverse.reshape(2 * M // LANES, LANES, Q)
    high, low = halves(inverse)
    to_planes = np.concatenate([high, high, low], axis=1)
    forward = np.stack([np.cos(angles), -np.sin(angles)], axis=1) / Q
    forward = forward.reshape(2 * M // LANES, LANES, Q).transpose(0, 2, 1)
    high, low = halves(forward)
    to_modes = np.concatenate([high, low], axis=2)
    return slopes, stiff, geometry.astype(np.float32), to_planes, to_modes


def split(values):
    high = values.astype(BF16)
    low = (values - high.astype(F32)).astype(BF16)
    return high, low


def dot(left, right):
    return jnp.dot(left, right, preferred_element_type=F32)


def kernel(
    grid_shape,
    slot_ref,
    lid_ref,
    vel_ref,
    slopes_hbm,
    stiff_hbm,
    geo_hbm,
    planes_hbm,
    modes_hbm,
    out_ref,
    vel,
    recv,
    slopes,
    stiff,
    geo,
    to_planes,
    to_modes,
    nodes,
    rhs,
    fields,
    planes,
    push_hi,
    push_lo,
    sendb,
    back,
    own,
    jac,
    vec,
    img,
    krhs,
    face_out,
    face_in,
    moment,
    red_a,
    red_b,
    local_sem,
    fwd_send,
    fwd_recv,
    bwd_send,
    bwd_recv,
    halo_send,
    halo_recv,
    a_send,
    a_recv,
    b_send,
    b_recv,
):
    ny, nz, nc = grid_shape
    n_elem = ny * nz * nc
    n_modes = ER
    mi = lax.axis_index("modes")
    e = lax.axis_index("elem")
    core = lax.rem(e, nc)
    zc = lax.rem(e // nc, nz)
    yc = e // (nc * nz)
    size_a = ny * nc
    rank_a = yc * nc + core

    def member_a(t):
        return ((t // nc) * nz + zc) * nc + lax.rem(t, nc)

    def member_b(t):
        return (yc * nz + t) * nc + core

    above = lax.rem(e + 1, n_elem)
    below = lax.rem(e + n_elem - 1, n_elem)

    local_pairs = [
        (vel_ref, vel),
        (slopes_hbm, slopes),
        (planes_hbm, to_planes),
        (geo_hbm, geo),
        (modes_hbm, to_modes),
        (stiff_hbm, stiff),
    ]
    local = [
        pltpu.make_async_copy(src, dst, local_sem.at[i]) for i, (src, dst) in enumerate(local_pairs)
    ]
    for copy in local:
        copy.start()

    barrier = pltpu.get_barrier_semaphore()
    greeted = [(lax.rem(mi + t, n_modes), e) for t in range(1, n_modes)]
    greeted += [(mi, above), (mi, below)]
    greeted += [(mi, member_a(lax.rem(rank_a + t, size_a))) for t in range(1, size_a)]
    greeted += [(mi, member_b(lax.rem(zc + t, nz))) for t in range(1, nz)]
    for who in greeted:
        pl.semaphore_signal(barrier, inc=1, device_id=who, device_id_type=MESH)
    pl.semaphore_wait(barrier, len(greeted))

    forward = {}
    for off in (2, 1, 3):
        to = lax.rem(mi + off, n_modes)
        forward[off] = pltpu.make_async_remote_copy(
            src_ref=vel_ref.at[:, to],
            dst_ref=recv.at[off],
            send_sem=fwd_send.at[off],
            recv_sem=fwd_recv.at[off],
            device_id=(to, e),
            device_id_type=MESH,
        )
        forward[off].start()

    lane = lax.broadcasted_iota(jnp.int32, (1, LANES), 1)
    even = lax.rem(lane, 2) == 0
    pair = (lane // 2).astype(F32)

    def times_unit(values):
        return jnp.where(even, -pltpu.roll(values, LANES - 1, 1), pltpu.roll(values, 1, 1))

    def pair_sum(values):
        return values + jnp.where(even, pltpu.roll(values, LANES - 1, 1), pltpu.roll(values, 1, 1))

    zero_rows = jnp.zeros((R - NODES + 4, LANES), F32)
    for s in range(3):
        nodes[s, NODES - 4 :, :] = zero_rows
        for g in range(ER):
            own[s, g, NODES - 4 :, :] = zero_rows
    no_rows = jnp.zeros((LANES - R, 3 * LANES), BF16)
    for part in range(3):
        rhs[part * LANES + R : (part + 1) * LANES, :] = no_rows
        for g in range(ER):
            krhs[g, part * LANES + R : (part + 1) * LANES, :] = no_rows
    moment[...] = jnp.zeros_like(moment)

    local[0].wait()
    for copy in local[1:3]:
        copy.wait()
    local[3].wait()

    cell = jnp.int32(0)
    for g in range(ER):
        cell = jnp.where(slot_ref[0, g] == mi, g, cell)
    radius = geo[3 * ER, :, :] + cell.astype(F32) * (1.0 / ER)
    inv_radius = 1.0 / radius
    swirl_base = SWIRL_SLOPE * radius + SWIRL_CURVE * inv_radius

    def add_modes(block, source, first):
        for s in range(3):
            for i in range(PS):
                nodes[s, PS * i : PS * (i + 1), :] = block(s, i)
        for s in range(3):
            high, low = split(nodes[s])
            cols = slice(s * LANES, (s + 1) * LANES)
            rhs[0:R, cols] = high
            rhs[LANES : LANES + R, cols] = low
            rhs[2 * LANES : 2 * LANES + R, cols] = high
        slope = dot(slopes[...], rhs[...])
        d_r = [slope[:R, s * LANES : (s + 1) * LANES] for s in range(3)]
        d_z = [slope[R:, s * LANES : (s + 1) * LANES] for s in range(3)]
        wave = pair + (source * (LANES // 2)).astype(F32)
        u_r, u_t, u_z = nodes[0], nodes[1], nodes[2]
        curl_r = wave * times_unit(u_z) * inv_radius - d_z[1]
        curl_t = d_z[0] - d_r[2]
        curl_z = d_r[1] + (u_t - wave * times_unit(u_r)) * inv_radius
        for f, values in enumerate((u_r, u_t, u_z, curl_r, curl_t, curl_z)):
            high, low = split(values)
            rows = slice(f * R, (f + 1) * R)
            fields[rows, 0:LANES] = high
            fields[rows, LANES : 2 * LANES] = low
            fields[rows, 2 * LANES :] = high
        terms = dot(fields[...], to_planes[source])
        if first:
            planes[...] = terms
        else:
            planes[...] += terms

    add_modes(lambda s, i: vel[s, mi, i], mi, True)

    for g in range(ER):
        held = slot_ref[0, g]
        for s in range(3):
            for i in range(PS):
                own[s, g, PS * i : PS * (i + 1), :] = vel[s, held, i]

    lid = lid_ref[...].astype(BF16)
    wide = lax.broadcasted_iota(jnp.int32, (LANES // 2, LANES), 1) // 2
    tall = lax.broadcasted_iota(jnp.int32, (LANES // 2, LANES), 0)
    noslip = dot(lid, (wide == tall).astype(BF16))
    side = geo[3 * ER + 1, :, :]
    low_side, high_side = side == 1.0, side == 2.0
    at_low, at_high = (e == 0).astype(F32), (e == n_elem - 1).astype(F32)
    lid_rows = jnp.where(low_side, at_low, 0.0) + jnp.where(high_side, at_high, 0.0)
    sharing = 1.0 + jnp.where(low_side, 1.0 - at_low, 0.0) + jnp.where(high_side, 1.0 - at_high, 0.0)
    wave_own = pair + (mi * (LANES // 2)).astype(F32)
    for s, offset in enumerate((1.0, -1.0, 0.0)):
        square = (wave_own + offset) * (wave_own + offset)
        lid_keep = 1.0 - lid_rows * (noslip if s < 2 else 1.0)
        for g in range(ER):
            fixed = geo[ER + g]
            diag = (fixed + square * geo[2 * ER + g]) * sharing
            jac[s, g] = jnp.where(fixed > 0.0, lid_keep / jnp.where(fixed > 0.0, diag, 1.0), 0.0)

    for off in (1, 3, 2):
        forward[off].wait_recv()
        source = lax.rem(mi + n_modes - off, n_modes)
        add_modes(lambda s, i: recv[off, s, i], source, False)

    block_rows = 16

    def push_rows(step, _):
        start = pl.multiple_of(step * block_rows, block_rows)

        def field(f, cols):
            return planes[pl.ds(pl.multiple_of(f * R + start, block_rows), block_rows), cols]

        geo_rows = geo[3 * ER, pl.ds(start, block_rows), :]
        rad = geo_rows + cell.astype(F32) * (1.0 / ER)
        swirl = SWIRL_SLOPE * rad + SWIRL_CURVE / rad
        swirl = jnp.concatenate([swirl] * 3, axis=1)
        spin = 2.0 * SWIRL_SLOPE
        for cols in (slice(0, 3 * LANES), slice(3 * LANES, 6 * LANES)):
            u_r, u_t, u_z, w_r, w_t, w_z = [field(f, cols) for f in range(6)]
            turned = u_t + swirl
            results = (
                turned * w_z - u_z * w_t + spin * u_t,
                u_z * w_r - u_r * w_z - spin * u_r,
                u_r * w_t - turned * w_r,
            )
            for s, values in enumerate(results):
                high, low = split(values)
                rows = pl.ds(pl.multiple_of(s * R + start, block_rows), block_rows)
                push_hi[rows, cols] = high
                push_lo[rows, cols] = low
        return 0

    lax.fori_loop(0, R // block_rows, push_rows, 0)

    local[4].wait()
    backward = {}
    for off in (2, 1, 3, 0):
        to = lax.rem(mi + off, n_modes)
        two = dot(push_hi[...], to_modes[to])
        one = dot(push_lo[...], to_modes[to, :, 0:LANES])
        result = two[:, :LANES] + (two[:, LANES:] + one)
        for s in range(3):
            if off == 0:
                back[mi, s] = result[s * R : (s + 1) * R]
            else:
                sendb[off, s] = result[s * R : (s + 1) * R]
        if off:
            backward[off] = pltpu.make_async_remote_copy(
                src_ref=sendb.at[off],
                dst_ref=back.at[mi],
                send_sem=bwd_send.at[off],
                recv_sem=bwd_recv.at[off],
                device_id=(to, e),
                device_id_type=MESH,
            )
            backward[off].start()
    local[5].wait()
    for off in (1, 3, 2):
        backward[off].wait_recv()

    for g in range(ER):
        held = slot_ref[0, g]
        force = [LAMBDA_COEF * own[s, g] + INV_NU * back[held, s] for s in range(3)]
        turned = times_unit(force[1])
        mass = geo[g]
        img[0, 0, g] = mass * (force[0] + turned)
        img[0, 1, g] = mass * (force[0] - turned)
        img[0, 2, g] = mass * force[2]

    face_row = lax.broadcasted_iota(jnp.int32, (ER * PS, 1), 0)
    inner_high = (lax.rem(face_row, PS) == PS - 1) & (face_row < ER * PS - 1)
    inner_low = (lax.rem(face_row, PS) == 0) & (face_row > 0)

    def low_rows():
        return pl.ds(0, PS, stride=PS)

    def high_rows():
        return pl.ds(PS - 1, PS, stride=PS)

    halos = []

    def send_faces(k):
        for s in range(3):
            for g in range(ER):
                rows = slice(g * PS, (g + 1) * PS)
                face_out[k, 0, s, rows, :] = img[k, s, g, low_rows(), :]
                face_out[k, 1, s, rows, :] = img[k, s, g, high_rows(), :]
        pairs = []
        for side_out, who in ((0, below), (1, above)):
            copy = pltpu.make_async_remote_copy(
                src_ref=face_out.at[k, side_out],
                dst_ref=face_in.at[k, 1 - side_out],
                send_sem=halo_send.at[k, side_out],
                recv_sem=halo_recv.at[k, 1 - side_out],
                device_id=(mi, who),
                device_id_type=MESH,
            )
            copy.start()
            pairs.append(copy)
        halos.append(pairs)

    def inner_part(k):
        for s in range(3):
            for g in range(ER):
                vec[k, s, g] = img[k, s, g]
            for g in range(ER - 1):
                shared = img[k, s, g, NODES - PS : NODES, :] + img[k, s, g + 1, 0:PS, :]
                vec[k, s, g, NODES - PS : NODES, :] = shared
                vec[k, s, g + 1, 0:PS, :] = shared
            for g in range(ER):
                vec[k, s, g] = vec[k, s, g] * jac[s, g]

    def outer_part(k):
        for copy in halos[k]:
            copy.wait_recv()
        for side_in, present, row_set in ((0, 1.0 - at_low, low_rows), (1, 1.0 - at_high, high_rows)):
            for s in range(3):
                values = face_in[k, side_in, s]
                values = values + jnp.where(inner_high, pltpu.roll(values, ER * PS - 1, 0), 0.0)
                after = face_in[k, side_in, s]
                values = values + jnp.where(inner_low, pltpu.roll(after, 1, 0), 0.0)
                values = values * present
                for g in range(ER):
                    part = values[g * PS : (g + 1) * PS] * jac[s, g, row_set(), :]
                    vec[k, s, g, row_set(), :] = vec[k, s, g, row_set(), :] + part

    def apply_stiff(k):
        for g in range(ER):
            for s in range(3):
                high, low = split(vec[k, s, g])
                cols = slice(s * LANES, (s + 1) * LANES)
                krhs[g, 0:R, cols] = high
                krhs[g, LANES : LANES + R, cols] = low
                krhs[g, 2 * LANES : 2 * LANES + R, cols] = high
            image = dot(stiff[g], krhs[g])
            for s in range(3):
                img[k + 1, s, g] = image[:, s * LANES : (s + 1) * LANES]

    def inner(k, left, right):
        for s in range(3):
            total = jnp.zeros((1, LANES), F32)
            for g in range(ER):
                products = vec[left, s, g] * img[right, s, g]
                total = total + jnp.sum(products, axis=0, keepdims=True)
            index = k * 3 + s
            moment[index // 9, index % 9 : index % 9 + 1, :] = total

    send_faces(0)
    inner_part(0)
    outer_part(0)
    apply_stiff(0)
    send_faces(1)
    inner(0, 0, 0)
    inner(1, 0, 1)
    inner_part(1)
    outer_part(1)
    apply_stiff(1)
    send_faces(2)
    inner(2, 1, 1)
    inner(3, 1, 2)
    inner_part(2)
    outer_part(2)
    apply_stiff(2)
    inner(4, 2, 2)
    inner(5, 2, 3)

    def exchange(buffer, rank, size, member, send_sems, recv_sems):
        copies = []
        for off in range(1, size):
            copy = pltpu.make_async_remote_copy(
                src_ref=buffer.at[rank],
                dst_ref=buffer.at[rank],
                send_sem=send_sems.at[off],
                recv_sem=recv_sems.at[off],
                device_id=(mi, member(lax.rem(rank + off, size))),
                device_id_type=MESH,
            )
            copy.start()
            copies.append(copy)
        for copy in copies:
            copy.wait_recv()
        total = buffer[0]
        for t in range(1, size):
            total = total + buffer[t]
        return total, copies

    red_a[rank_a] = jnp.where(even, pair_sum(moment[0]), pair_sum(moment[1]))
    total, copies_a = exchange(red_a, rank_a, size_a, member_a, a_send, a_recv)
    red_b[zc] = total
    total, copies_b = exchange(red_b, zc, nz, member_b, b_send, b_recv)
    first = jnp.where(even, total, pltpu.roll(total, 1, 1))
    second = jnp.where(even, pltpu.roll(total, LANES - 1, 1), total)

    coefs = []
    for s in range(3):
        h = [(first if k < 3 else second)[(k % 3) * 3 + s : (k % 3) * 3 + s + 1] for k in range(6)]
        g00, g01, g02, g12, g22 = [h[k] + h[k + 1] for k in range(5)]
        g11 = g02
        ratio1, ratio2 = g01 / g00, g02 / g00
        d1 = g11 - ratio1 * g01
        left = g12 - ratio1 * g02
        ratio = left / d1
        d2 = g22 - ratio2 * g02 - ratio * left
        y1 = h[1] - ratio1 * h[0]
        y2 = h[2] - ratio2 * h[0] - ratio * y1
        c2 = y2 / d2
        c1 = y1 / d1 - ratio * c2
        c0 = h[0] / g00 - ratio1 * c1 - ratio2 * c2
        coefs.append((c0, c1, c2))

    for slot in range(ER):
        held = jnp.int32(0)
        for g in range(ER):
            held = jnp.where(slot_ref[0, g] == slot, g, held)
        plus, minus, axial = [
            coefs[s][0] * vec[0, s, held] + coefs[s][1] * vec[1, s, held] + coefs[s][2] * vec[2, s, held]
            for s in range(3)
        ]
        results = ((plus + minus) * 0.5, times_unit(minus - plus) * 0.5, axial)
        for s, values in enumerate(results):
            for i in range(PS):
                out_ref[s, slot, i] = values[PS * i : PS * (i + 1)]

    for copies in (forward.values(), backward.values(), copies_a, copies_b, *halos):
        for copy in copies:
            copy.wait_send()


def on_device(grid_shape, velocity, element_slot, lid_noslip):
    ny, nz, nc = grid_shape
    slopes, stiff, geometry, to_planes, to_modes = constants()
    any_spec = pl.BlockSpec(memory_space=pl.ANY)
    vmem = pltpu.VMEM
    dma = pltpu.SemaphoreType.DMA
    return pl.pallas_call(
        functools.partial(kernel, grid_shape),
        out_shape=jax.ShapeDtypeStruct(velocity.shape, F32),
        in_specs=[
            pl.BlockSpec(memory_space=pltpu.SMEM),
            pl.BlockSpec(memory_space=vmem),
        ]
        + [any_spec] * 6,
        out_specs=pl.BlockSpec(memory_space=vmem),
        scratch_shapes=[
            vmem(velocity.shape, F32),
            vmem((ER, 3, PS, PS, LANES), F32),
            vmem(slopes.shape, BF16),
            vmem(stiff.shape, BF16),
            vmem(geometry.shape, F32),
            vmem(to_planes.shape, BF16),
            vmem(to_modes.shape, BF16),
            vmem((3, R, LANES), F32),
            vmem((3 * LANES, 3 * LANES), BF16),
            vmem((6 * R, 3 * LANES), BF16),
            vmem((6 * R, Q), F32),
            vmem((3 * R, Q), BF16),
            vmem((3 * R, Q), BF16),
            vmem((ER, 3, R, LANES), F32),
            vmem((ER, 3, R, LANES), F32),
            vmem((3, ER, R, LANES), F32),
            vmem((3, ER, R, LANES), F32),
            vmem((3, 3, ER, R, LANES), F32),
            vmem((4, 3, ER, R, LANES), F32),
            vmem((ER, 3 * LANES, 3 * LANES), BF16),
            vmem((3, 2, 3, ER * PS, LANES), F32),
            vmem((3, 2, 3, ER * PS, LANES), F32),
            vmem((2, 16, LANES), F32),
            vmem((ny * nc, 16, LANES), F32),
            vmem((nz, 16, LANES), F32),
            dma((6,)),
            dma((ER,)),
            dma((ER,)),
            dma((ER,)),
            dma((ER,)),
            dma((3, 2)),
            dma((3, 2)),
            dma((ny * nc,)),
            dma((ny * nc,)),
            dma((nz,)),
            dma((nz,)),
        ],
        compiler_params=pltpu.CompilerParams(
            collective_id=0, has_side_effects=True, vmem_limit_bytes=48 * 1024 * 1024
        ),
    )(
        element_slot,
        lid_noslip.reshape(1, -1),
        velocity,
        jnp.asarray(slopes),
        jnp.asarray(stiff),
        jnp.asarray(geometry),
        jnp.asarray(to_planes),
        jnp.asarray(to_modes),
    )


def solution(mesh):
    n_elem = mesh.shape["elem"]
    nc = 2
    nz = min(8, n_elem // nc)
    ny = n_elem // (nc * nz)
    return jax.shard_map(
        functools.partial(on_device, (ny, nz, nc)),
        mesh=mesh,
        in_specs=(P(None, "elem", None, None, "modes"), P("elem", None), P("modes")),
        out_specs=P(None, "elem", None, None, "modes"),
        check_vma=False,
    )
```

time: 1000 us -> 61.8 us (0.06)
  blocking collectives: 623 us -> 0 us
  other arithmetic: 156 us -> 0 us
  local copies, waits for them, and re-layouts: 126 us -> 7.15 us
  Pallas kernels: 0 us -> 54.4 us
  starting transfers between devices: 36.3 us -> 0 us
  matrix products: 28.1 us -> 0 us
  waiting for transfers between devices: 20.1 us -> 0 us
    psum x5 -> x0, blocking collectives: 623 us -> none  [global_inner(): return lax.psum(mode_inner(left_vec, right_vec, inv_mult), 'elem')]
    unnamed x1 -> x0, other arithmetic: 72.3 us -> none
    pallas_call x0 -> x1, Pallas kernels: none -> 54.4 us  [on_device(): pl.pallas_call(functools.partial(kernel, grid_shape), out_shape=jax.Shape...]
    dot_general x22 -> x0, matrix products: 28.1 us -> none  [the longest x1 4.98 us: plane_products(): jnp.dot(stacked, inverse_table, precision=highest).reshape(6, row_count, -1)]
    unnamed x60 -> x13, local copies, waits for them, and re-layouts: 33.2 us -> 5.93 us
    another operation x21 -> x0, other arithmetic: 27.2 us -> none  [the longest x3 12.1 us: times_unit(): jnp.stack([-pair_view[..., 1], pair_view[..., 0]], axis=-1)]
    ppermute x8 -> x0, starting transfers between devices: 22.8 us -> none  [the longest x4 13.1 us: extended(): lax.ppermute(lax.slice_in_dim(block, block.shape[dim] - width, None, axis...]
    all_to_all x3 -> x0, local copies, waits for them, and re-layouts: 16.4 us -> none  [the longest x1 14.2 us: on_device(): lax.all_to_all(pushed_hat, 'modes', split_axis=5, concat_axis=1, tiled=True)]
  transfers between devices with their start and end apart: 11 -> 0, of which waited for: 7 -> 0; matrix products, arithmetic and copies ran while one was open for 4% -> 0% of each run, Pallas kernels for 0% -> 0%
where the time goes in v1:
time: 61.8 us; the launch traced here: 61.6 us
  Pallas kernels  54.4 us (88%)
  local copies, waits for them, and re-layouts  7.15 us (12%)
    pallas_call x1, Pallas kernels, on_device(): pl.pallas_call(functools.partial(kernel, grid_shape), out_shape=jax.Shape...  54.4 us
    unnamed x13, local copies, waits for them, and re-layouts  5.93 us

profile of v1, /device:TPU:1, one launch (start us, length us, event | category | flops | bytes accessed | tf_op | source)
XLA Modules:
  0.0 61.6 jit_solution(8498008029360656878)
XLA Ops:
  0.0 0.0 copy-start
  0.0 1.3 %copy.9.vel_ref = f32[3,4,10,10,128]{4,3,2,1,0:T(8,128)S(1)} copy(f32[3,4,10,10,128]{4,1,3,2,0:T(4,128)} %param.8) | data formatting | bytes 1228800 | tf_op args[0]
  1.3 0.3 copy-done
  1.6 0.0 copy-start.1
  1.6 1.1 %copy-done.1 = f32[14,112,128]{2,1,0:T(8,128)S(1)} copy-done((f32[14,112,128]{2,1,0:T(8,128)S(1)}, f32[14,112,128]{2,1,0:T(8,128)}, u32[]{:S(2)}) %copy-start.1) | copy-done | bytes 802840
  2.7 0.0 copy-start.2
  2.7 1.0 %copy-done.2 = bf16[4,112,384]{2,1,0:T(8,128)(2,1)S(1)} copy-done((bf16[4,112,384]{2,1,0:T(8,128)(2,1)S(1)}, bf16[4,112,384]{2,1,0:T(8,128)(2,1)}, u32[]{:S(2)}) %copy-start.2) | copy-done | bytes 344088
  3.7 0.0 copy-start.3
  3.7 0.9 %copy-done.3 = bf16[224,384]{1,0:T(8,128)(2,1)S(1)} copy-done((bf16[224,384]{1,0:T(8,128)(2,1)S(1)}, bf16[224,384]{1,0:T(8,128)(2,1)}, u32[]{:S(2)}) %copy-start.3) | copy-done | bytes 172056
  4.6 0.0 copy-start.4
  4.6 0.7 %copy-done.4 = s32[1,4]{1,0:T(1,128)S(1)} copy-done((s32[1,4]{1,0:T(1,128)S(1)}, s32[1,4]{1,0:T(1,128)}, u32[]{:S(2)}) %copy-start.4) | copy-done | bytes 40
  5.3 0.0 copy-start.5
  5.3 0.7 %copy-done.5 = s32[64]{0:T(128)S(1)} copy-done((s32[64]{0:T(128)S(1)}, s32[64]{0:T(128)}, u32[]{:S(2)}) %copy-start.5) | copy-done | bytes 280
  5.9 54.4 %shard_map.82 = f32[3,4,10,10,128]{4,3,2,1,0:T(8,128)S(1)} custom-call(s32[1,4]{1,0:T(1,128)S(1)} %copy-done.4, s32[1,64]{1,0:T(1,128)S(1)} %bitcast.1, f32[3,4,10,10,128]{4,3,2,1,0:T(8,128)S(1)} %copy.9.vel_ref, bf16[224,384]{1,0:T(8,128)(2,1)S(1)} %copy-done.3, bf16[4,112,384]{2,1,0:T(8,128)(2,1)S(1)} %copy-done.2, f32[14,112,128]{2,1,0:T(8,128)S(1)} %copy-done.1, ...), custom_call_target="tpu_custom_call" | custom-call | tf_op jit(solution)/shard_map/pallas_call | solution.py:569
  60.4 1.2 %copy.10 = f32[3,4,10,10,128]{4,1,3,2,0:T(4,128)} copy(f32[3,4,10,10,128]{4,3,2,1,0:T(8,128)S(1)} %shard_map.82) | data formatting | bytes 1228800 | tf_op jit(solution)/shard_map/pallas_call | solution.py:569
Async XLA Ops:
  0.0 1.6 %copy-start = (bf16[4,768,256]{2,1,0:T(8,128)(2,1)S(1)}, bf16[4,768,256]{2,1,0:T(8,128)(2,1)}, u32[]{:S(2)}) copy-start(bf16[4,768,256]{2,1,0:T(8,128)(2,1)} %constant.14.clone.modes_hbm) | copy-start | bytes 4718596
  1.6 1.1 %copy-start.1 = (f32[14,112,128]{2,1,0:T(8,128)S(1)}, f32[14,112,128]{2,1,0:T(8,128)}, u32[]{:S(2)}) copy-start(f32[14,112,128]{2,1,0:T(8,128)} %constant.12.clone.geo_hbm) | copy-start | bytes 2408452
  2.7 1.0 %copy-start.2 = (bf16[4,112,384]{2,1,0:T(8,128)(2,1)S(1)}, bf16[4,112,384]{2,1,0:T(8,128)(2,1)}, u32[]{:S(2)}) copy-start(bf16[4,112,384]{2,1,0:T(8,128)(2,1)} %constant.11.clone.stiff_hbm) | copy-start | bytes 1032196
  3.7 0.9 %copy-start.3 = (bf16[224,384]{1,0:T(8,128)(2,1)S(1)}, bf16[224,384]{1,0:T(8,128)(2,1)}, u32[]{:S(2)}) copy-start(bf16[224,384]{1,0:T(8,128)(2,1)} %constant.10.clone.slopes_hbm) | copy-start | bytes 516100
  4.6 0.7 %copy-start.4 = (s32[1,4]{1,0:T(1,128)S(1)}, s32[1,4]{1,0:T(1,128)}, u32[]{:S(2)}) copy-start(s32[1,4]{1,0:T(1,128)} %slot_ref.1) | copy-start | bytes 52
  5.3 0.7 %copy-start.5 = (s32[64]{0:T(128)S(1)}, s32[64]{0:T(128)}, u32[]{:S(2)}) copy-start(s32[64]{0:T(128)} %param.10) | copy-start | bytes 772

commit v2 on v1

--- a/solution.py
+++ b/solution.py
@@ -139,23 +139,25 @@
 
 def kernel(
     grid_shape,
-    slot_ref,
-    lid_ref,
-    vel_ref,
+    slot_hbm,
+    lid_hbm,
+    vel_hbm,
     slopes_hbm,
     stiff_hbm,
     geo_hbm,
     planes_hbm,
     modes_hbm,
     out_ref,
+    slot_ref,
+    lid_ref,
     vel,
+    slots,
     recv,
     slopes,
     stiff,
     geo,
     to_planes,
     to_modes,
-    nodes,
     rhs,
     fields,
     planes,
@@ -163,7 +165,6 @@
     push_lo,
     sendb,
     back,
-    own,
     jac,
     vec,
     img,
@@ -206,10 +207,12 @@
     below = lax.rem(e + n_elem - 1, n_elem)
 
     local_pairs = [
-        (vel_ref, vel),
+        (vel_hbm, vel),
         (slopes_hbm, slopes),
         (planes_hbm, to_planes),
         (geo_hbm, geo),
+        (slot_hbm, slot_ref),
+        (lid_hbm, lid_ref),
         (modes_hbm, to_modes),
         (stiff_hbm, stiff),
     ]
@@ -219,6 +222,21 @@
     for copy in local:
         copy.start()
 
+    for g in range(ER):
+        for s in range(3):
+            slots[g, s, R - 16 :, :] = jnp.zeros((16, LANES), F32)
+    no_rows = jnp.zeros((LANES - R, 3 * LANES), BF16)
+    for part in range(3):
+        rhs[part * LANES + R : (part + 1) * LANES, :] = no_rows
+        for g in range(ER):
+            krhs[g, part * LANES + R : (part + 1) * LANES, :] = no_rows
+    moment[...] = jnp.zeros_like(moment)
+
+    def gather_slot(slot):
+        for s in range(3):
+            rows = pl.ds(s * NODES * ER + slot, NODES, stride=ER)
+            slots[slot, s, 0:NODES, :] = vel[rows, :]
+
     barrier = pltpu.get_barrier_semaphore()
     greeted = [(lax.rem(mi + t, n_modes), e) for t in range(1, n_modes)]
     greeted += [(mi, above), (mi, below)]
@@ -228,11 +246,13 @@
         pl.semaphore_signal(barrier, inc=1, device_id=who, device_id_type=MESH)
     pl.semaphore_wait(barrier, len(greeted))
 
+    local[0].wait()
     forward = {}
     for off in (2, 1, 3):
         to = lax.rem(mi + off, n_modes)
+        gather_slot(to)
         forward[off] = pltpu.make_async_remote_copy(
-            src_ref=vel_ref.at[:, to],
+            src_ref=slots.at[to],
             dst_ref=recv.at[off],
             send_sem=fwd_send.at[off],
             recv_sem=fwd_recv.at[off],
@@ -251,22 +271,9 @@
     def pair_sum(values):
         return values + jnp.where(even, pltpu.roll(values, LANES - 1, 1), pltpu.roll(values, 1, 1))
 
-    zero_rows = jnp.zeros((R - NODES + 4, LANES), F32)
-    for s in range(3):
-        nodes[s, NODES - 4 :, :] = zero_rows
-        for g in range(ER):
-            own[s, g, NODES - 4 :, :] = zero_rows
-    no_rows = jnp.zeros((LANES - R, 3 * LANES), BF16)
-    for part in range(3):
-        rhs[part * LANES + R : (part + 1) * LANES, :] = no_rows
-        for g in range(ER):
-            krhs[g, part * LANES + R : (part + 1) * LANES, :] = no_rows
-    moment[...] = jnp.zeros_like(moment)
-
-    local[0].wait()
-    for copy in local[1:3]:
+    gather_slot(mi)
+    for copy in local[1:6]:
         copy.wait()
-    local[3].wait()
 
     cell = jnp.int32(0)
     for g in range(ER):
@@ -277,10 +284,7 @@
 
     def add_modes(block, source, first):
         for s in range(3):
-            for i in range(PS):
-                nodes[s, PS * i : PS * (i + 1), :] = block(s, i)
-        for s in range(3):
-            high, low = split(nodes[s])
+            high, low = split(block[s])
             cols = slice(s * LANES, (s + 1) * LANES)
             rhs[0:R, cols] = high
             rhs[LANES : LANES + R, cols] = low
@@ -289,7 +293,7 @@
         d_r = [slope[:R, s * LANES : (s + 1) * LANES] for s in range(3)]
         d_z = [slope[R:, s * LANES : (s + 1) * LANES] for s in range(3)]
         wave = pair + (source * (LANES // 2)).astype(F32)
-        u_r, u_t, u_z = nodes[0], nodes[1], nodes[2]
+        u_r, u_t, u_z = block[0], block[1], block[2]
         curl_r = wave * times_unit(u_z) * inv_radius - d_z[1]
         curl_t = d_z[0] - d_r[2]
         curl_z = d_r[1] + (u_t - wave * times_unit(u_r)) * inv_radius
@@ -305,13 +309,7 @@
         else:
             planes[...] += terms
 
-    add_modes(lambda s, i: vel[s, mi, i], mi, True)
-
-    for g in range(ER):
-        held = slot_ref[0, g]
-        for s in range(3):
-            for i in range(PS):
-                own[s, g, PS * i : PS * (i + 1), :] = vel[s, held, i]
+    add_modes(slots.at[mi], mi, True)
 
     lid = lid_ref[...].astype(BF16)
     wide = lax.broadcasted_iota(jnp.int32, (LANES // 2, LANES), 1) // 2
@@ -334,7 +332,7 @@
     for off in (1, 3, 2):
         forward[off].wait_recv()
         source = lax.rem(mi + n_modes - off, n_modes)
-        add_modes(lambda s, i: recv[off, s, i], source, False)
+        add_modes(recv.at[off], source, False)
 
     block_rows = 16
 
@@ -366,7 +364,7 @@
 
     lax.fori_loop(0, R // block_rows, push_rows, 0)
 
-    local[4].wait()
+    local[6].wait()
     backward = {}
     for off in (2, 1, 3, 0):
         to = lax.rem(mi + off, n_modes)
@@ -388,13 +386,13 @@
                 device_id_type=MESH,
             )
             backward[off].start()
-    local[5].wait()
+    local[7].wait()
     for off in (1, 3, 2):
         backward[off].wait_recv()
 
     for g in range(ER):
         held = slot_ref[0, g]
-        force = [LAMBDA_COEF * own[s, g] + INV_NU * back[held, s] for s in range(3)]
+        force = [LAMBDA_COEF * slots[held, s] + INV_NU * back[held, s] for s in range(3)]
         turned = times_unit(force[1])
         mass = geo[g]
         img[0, 0, g] = mass * (force[0] + turned)
@@ -552,8 +550,8 @@
         ]
         results = ((plus + minus) * 0.5, times_unit(minus - plus) * 0.5, axial)
         for s, values in enumerate(results):
-            for i in range(PS):
-                out_ref[s, slot, i] = values[PS * i : PS * (i + 1)]
+            rows = pl.ds(s * NODES * ER + slot, NODES, stride=ER)
+            out_ref[rows, :] = values[:NODES]
 
     for copies in (forward.values(), backward.values(), copies_a, copies_b, *halos):
         for copy in copies:
@@ -563,27 +561,25 @@
 def on_device(grid_shape, velocity, element_slot, lid_noslip):
     ny, nz, nc = grid_shape
     slopes, stiff, geometry, to_planes, to_modes = constants()
-    any_spec = pl.BlockSpec(memory_space=pl.ANY)
     vmem = pltpu.VMEM
     dma = pltpu.SemaphoreType.DMA
-    return pl.pallas_call(
+    flat = velocity.transpose(0, 2, 3, 1, 4).reshape(3 * NODES * ER, LANES)
+    result = pl.pallas_call(
         functools.partial(kernel, grid_shape),
-        out_shape=jax.ShapeDtypeStruct(velocity.shape, F32),
-        in_specs=[
-            pl.BlockSpec(memory_space=pltpu.SMEM),
-            pl.BlockSpec(memory_space=vmem),
-        ]
-        + [any_spec] * 6,
+        out_shape=jax.ShapeDtypeStruct((3 * NODES * ER, LANES), F32),
+        in_specs=[pl.BlockSpec(memory_space=pltpu.HBM)] * 8,
         out_specs=pl.BlockSpec(memory_space=vmem),
         scratch_shapes=[
-            vmem(velocity.shape, F32),
-            vmem((ER, 3, PS, PS, LANES), F32),
+            pltpu.SMEM((1, ER), jnp.int32),
+            vmem((1, LANES // 2), jnp.int32),
+            vmem((3 * NODES * ER, LANES), F32),
+            vmem((ER, 3, R, LANES), F32),
+            vmem((ER, 3, R, LANES), F32),
             vmem(slopes.shape, BF16),
             vmem(stiff.shape, BF16),
             vmem(geometry.shape, F32),
             vmem(to_planes.shape, BF16),
             vmem(to_modes.shape, BF16),
-            vmem((3, R, LANES), F32),
             vmem((3 * LANES, 3 * LANES), BF16),
             vmem((6 * R, 3 * LANES), BF16),
             vmem((6 * R, Q), F32),
@@ -591,7 +587,6 @@
             vmem((3 * R, Q), BF16),
             vmem((ER, 3, R, LANES), F32),
             vmem((ER, 3, R, LANES), F32),
-            vmem((3, ER, R, LANES), F32),
             vmem((3, ER, R, LANES), F32),
             vmem((3, 3, ER, R, LANES), F32),
             vmem((4, 3, ER, R, LANES), F32),
@@ -601,7 +596,7 @@
             vmem((2, 16, LANES), F32),
             vmem((ny * nc, 16, LANES), F32),
             vmem((nz, 16, LANES), F32),
-            dma((6,)),
+            dma((8,)),
             dma((ER,)),
             dma((ER,)),
             dma((ER,)),
@@ -614,18 +609,19 @@
             dma((nz,)),
         ],
         compiler_params=pltpu.CompilerParams(
-            collective_id=0, has_side_effects=True, vmem_limit_bytes=48 * 1024 * 1024
+            collective_id=0, has_side_effects=True, vmem_limit_bytes=62 * 1024 * 1024
         ),
     )(
         element_slot,
         lid_noslip.reshape(1, -1),
-        velocity,
+        flat,
         jnp.asarray(slopes),
         jnp.asarray(stiff),
         jnp.asarray(geometry),
         jnp.asarray(to_planes),
         jnp.asarray(to_modes),
     )
+    return result.reshape(3, PS, PS, ER, LANES).transpose(0, 3, 1, 2, 4)
 
 
 def solution(mesh):

time: 61.8 us -> 56.9 us (0.921)
  local copies, waits for them, and re-layouts: 7.15 us -> 1.94 us
    unnamed x13 -> x1, local copies, waits for them, and re-layouts: 5.93 us -> 1.94 us
    pallas_call x1 -> x0, local copies, waits for them, and re-layouts: 1.22 us -> none  [on_device(): pl.pallas_call(functools.partial(kernel, grid_shape), out_shape=jax.Shape...]
where the time goes in v2:
time: 56.9 us; the launch traced here: 56.8 us
  Pallas kernels  54.8 us (96%)
  local copies, waits for them, and re-layouts  1.94 us (3%)
    pallas_call x1, Pallas kernels, on_device(): pl.pallas_call(functools.partial(kernel, grid_shape), out_shape=jax.Shape...  54.8 us
    unnamed x1, local copies, waits for them, and re-layouts  1.94 us

profile of v2, /device:TPU:1, one launch (start us, length us, event | category | flops | bytes accessed | tf_op | source)
XLA Modules:
  0.0 56.8 jit_solution(15367431780291859478)
XLA Ops:
  0.0 54.8 %shard_map.82 = f32[1200,128]{1,0:T(8,128)} custom-call(s32[1,4]{1,0:T(1,128)} %slot_hbm.1, s32[1,64]{1,0:T(1,128)} %bitcast.9, f32[1200,128]{1,0:T(8,128)} %bitcast.8, bf16[224,384]{1,0:T(8,128)(2,1)} %constant.10.clone.slopes_hbm, bf16[4,112,384]{2,1,0:T(8,128)(2,1)} %constant.11.clone.stiff_hbm, f32[14,112,128]{2,1,0:T(8,128)} %constant.12.clone.geo_hbm, ...), custom_call_target="tpu_custom_call" | custom-call | tf_op jit(solution)/shard_map/pallas_call | solution.py:567
  54.8 1.9 %copy.10 = f32[3,4,10,10,128]{4,1,3,2,0:T(4,128)} copy(f32[3,4,10,10,128]{4,1,3,2,0:T(4,128)} %bitcast.7) | data formatting | bytes 1228800

commit v3 on v2

--- a/solution.py
+++ b/solution.py
@@ -12,6 +12,11 @@
 PS = 10
 NODES = PS * PS
 R = 112
+SENT = 104
+TOP = 88
+FACE = 16
+MID = TOP - FACE
+BULK = 80
 M = 256
 Q = 768
 ER = 4
@@ -74,16 +79,16 @@
         high, low = halves(padded)
         return np.concatenate([high, high, low], axis=1)
 
-    slope_r = operator(2.0 * ER * np.kron(deriv, eye))
-    slope_z = operator(2.0 * ER * np.kron(eye, deriv))
+    slope_r = operator(2.0 * ER * np.kron(eye, deriv))
+    slope_z = operator(2.0 * ER * np.kron(deriv, eye))
     slopes = np.concatenate([slope_r, slope_z], axis=0)
 
     stiff, stiff_diag = [], np.zeros((ER, PS, PS))
     for ir in range(ER):
         along_i = deriv.T @ np.diag(w * radius[ir]) @ deriv
         along_j = deriv.T @ np.diag(w) @ deriv
-        whole = np.kron(along_i, np.diag(w)) + np.kron(np.diag(w * radius[ir]), along_j)
-        stiff_diag[ir] = np.diag(whole).reshape(PS, PS)
+        whole = np.kron(np.diag(w), along_i) + np.kron(along_j, np.diag(w * radius[ir]))
+        stiff_diag[ir] = np.diag(whole).reshape(PS, PS).T
         stiff.append(operator(whole - np.diag(np.diag(whole))))
     stiff = np.stack(stiff)
 
@@ -103,15 +108,13 @@
     diag_fixed[-1, -1] = 0.0
 
     geometry = np.zeros((3 * ER + 2, R, LANES))
-    geometry[0:ER, :NODES] = mass_r.reshape(ER, NODES, 1)
-    geometry[ER : 2 * ER, :NODES] = diag_fixed.reshape(ER, NODES, 1)
-    geometry[2 * ER : 3 * ER, :NODES] = diag_square.reshape(ER, NODES, 1)
+    for part, values in enumerate((mass_r, diag_fixed, diag_square)):
+        rows = values.transpose(0, 2, 1).reshape(ER, NODES, 1)
+        geometry[part * ER : (part + 1) * ER, :NODES] = rows
     geometry[3 * ER] = 1.0
-    geometry[3 * ER, :NODES] = (R_INNER + 0.5 * (np.repeat(xi, PS) + 1.0) / ER)[:, None]
-    face = np.zeros((PS, PS))
-    face[:, 0] = 1.0
-    face[:, -1] = 2.0
-    geometry[3 * ER + 1, :NODES] = face.reshape(NODES, 1)
+    geometry[3 * ER, :NODES] = (R_INNER + 0.5 * (np.tile(xi, PS) + 1.0) / ER)[:, None]
+    geometry[3 * ER + 1, :PS] = 1.0
+    geometry[3 * ER + 1, NODES - PS : NODES] = 2.0
 
     modes = np.arange(M)
     angles = (modes[:, None] * np.arange(Q)[None, :] % Q) * (2.0 * np.pi / Q)
@@ -150,8 +153,10 @@
     out_ref,
     slot_ref,
     lid_ref,
-    vel,
-    slots,
+    vel_r,
+    vel_t,
+    vel_z,
+    cells,
     recv,
     slopes,
     stiff,
@@ -163,13 +168,18 @@
     planes,
     push_hi,
     push_lo,
+    side_hi,
+    side_lo,
     sendb,
     back,
+    side_out,
+    side_in,
+    side_send,
+    side_back,
     jac,
     vec,
     img,
     krhs,
-    face_out,
     face_in,
     moment,
     red_a,
@@ -179,6 +189,9 @@
     fwd_recv,
     bwd_send,
     bwd_recv,
+    side_sems,
+    fb_send,
+    fb_recv,
     halo_send,
     halo_recv,
     a_send,
@@ -206,8 +219,13 @@
     above = lax.rem(e + 1, n_elem)
     below = lax.rem(e + n_elem - 1, n_elem)
 
+    span = NODES * ER
+    vel = (vel_r, vel_t, vel_z)
     local_pairs = [
-        (vel_hbm, vel),
+        *[
+            (vel_hbm.at[pl.ds(s * span, span)], vel[s])
+            for s in range(3)
+        ],
         (slopes_hbm, slopes),
         (planes_hbm, to_planes),
         (geo_hbm, geo),
@@ -224,7 +242,9 @@
 
     for g in range(ER):
         for s in range(3):
-            slots[g, s, R - 16 :, :] = jnp.zeros((16, LANES), F32)
+            cells[g, s, R - 16 :, :] = jnp.zeros((16, LANES), F32)
+            recv[g, s, R - 16 :, :] = jnp.zeros((16, LANES), F32)
+            img[0, s, g, SENT:, :] = jnp.zeros((R - SENT, LANES), F32)
     no_rows = jnp.zeros((LANES - R, 3 * LANES), BF16)
     for part in range(3):
         rhs[part * LANES + R : (part + 1) * LANES, :] = no_rows
@@ -232,10 +252,11 @@
             krhs[g, part * LANES + R : (part + 1) * LANES, :] = no_rows
     moment[...] = jnp.zeros_like(moment)
 
-    def gather_slot(slot):
-        for s in range(3):
-            rows = pl.ds(s * NODES * ER + slot, NODES, stride=ER)
-            slots[slot, s, 0:NODES, :] = vel[rows, :]
+    def gather_cell(g, s, target):
+        held = slot_ref[0, g]
+        for j in range(PS):
+            rows = pl.ds(j * ER + held, PS, stride=ER * PS)
+            target[g, s, j * PS : (j + 1) * PS, :] = vel[s][rows, :]
 
     barrier = pltpu.get_barrier_semaphore()
     greeted = [(lax.rem(mi + t, n_modes), e) for t in range(1, n_modes)]
@@ -246,20 +267,22 @@
         pl.semaphore_signal(barrier, inc=1, device_id=who, device_id_type=MESH)
     pl.semaphore_wait(barrier, len(greeted))
 
-    local[0].wait()
     forward = {}
-    for off in (2, 1, 3):
-        to = lax.rem(mi + off, n_modes)
-        gather_slot(to)
-        forward[off] = pltpu.make_async_remote_copy(
-            src_ref=slots.at[to],
-            dst_ref=recv.at[off],
-            send_sem=fwd_send.at[off],
-            recv_sem=fwd_recv.at[off],
-            device_id=(to, e),
-            device_id_type=MESH,
-        )
-        forward[off].start()
+    local[6].wait()
+    for s in range(3):
+        local[s].wait()
+        for off in (2, 1, 3):
+            to = lax.rem(mi + off, n_modes)
+            gather_cell(to, s, cells)
+            forward[off, s] = pltpu.make_async_remote_copy(
+                src_ref=cells.at[to, s, pl.ds(0, SENT)],
+                dst_ref=recv.at[mi, s, pl.ds(0, SENT)],
+                send_sem=fwd_send.at[off, s],
+                recv_sem=fwd_recv.at[off, s],
+                device_id=(to, e),
+                device_id_type=MESH,
+            )
+            forward[off, s].start()
 
     lane = lax.broadcasted_iota(jnp.int32, (1, LANES), 1)
     even = lax.rem(lane, 2) == 0
@@ -271,14 +294,13 @@
     def pair_sum(values):
         return values + jnp.where(even, pltpu.roll(values, LANES - 1, 1), pltpu.roll(values, 1, 1))
 
-    gather_slot(mi)
-    for copy in local[1:6]:
+    for s in range(3):
+        gather_cell(mi, s, recv)
+    for copy in (*local[3:6], local[7]):
         copy.wait()
 
-    cell = jnp.int32(0)
-    for g in range(ER):
-        cell = jnp.where(slot_ref[0, g] == mi, g, cell)
-    radius = geo[3 * ER, :, :] + cell.astype(F32) * (1.0 / ER)
+    cell_radius = mi.astype(F32) * (1.0 / ER)
+    radius = geo[3 * ER, :, :] + cell_radius
     inv_radius = 1.0 / radius
     swirl_base = SWIRL_SLOPE * radius + SWIRL_CURVE * inv_radius
 
@@ -309,7 +331,7 @@
         else:
             planes[...] += terms
 
-    add_modes(slots.at[mi], mi, True)
+    add_modes(recv.at[mi], mi, True)
 
     lid = lid_ref[...].astype(BF16)
     wide = lax.broadcasted_iota(jnp.int32, (LANES // 2, LANES), 1) // 2
@@ -330,20 +352,16 @@
             jac[s, g] = jnp.where(fixed > 0.0, lid_keep / jnp.where(fixed > 0.0, diag, 1.0), 0.0)
 
     for off in (1, 3, 2):
-        forward[off].wait_recv()
+        for s in range(3):
+            forward[off, s].wait_recv()
         source = lax.rem(mi + n_modes - off, n_modes)
-        add_modes(recv.at[off], source, False)
-
-    block_rows = 16
-
-    def push_rows(step, _):
-        start = pl.multiple_of(step * block_rows, block_rows)
-
+        add_modes(recv.at[source], source, False)
+
+    def push_rows(start, to_hi, to_lo, first, pitch):
         def field(f, cols):
-            return planes[pl.ds(pl.multiple_of(f * R + start, block_rows), block_rows), cols]
-
-        geo_rows = geo[3 * ER, pl.ds(start, block_rows), :]
-        rad = geo_rows + cell.astype(F32) * (1.0 / ER)
+            return planes[pl.ds(pl.multiple_of(f * R + start, 8), FACE), cols]
+
+        rad = geo[3 * ER, pl.ds(start, FACE), :] + cell_radius
         swirl = SWIRL_SLOPE * rad + SWIRL_CURVE / rad
         swirl = jnp.concatenate([swirl] * 3, axis=1)
         spin = 2.0 * SWIRL_SLOPE
@@ -357,73 +375,131 @@
             )
             for s, values in enumerate(results):
                 high, low = split(values)
-                rows = pl.ds(pl.multiple_of(s * R + start, block_rows), block_rows)
-                push_hi[rows, cols] = high
-                push_lo[rows, cols] = low
+                rows = pl.ds(pl.multiple_of(first + s * pitch, FACE), FACE)
+                to_hi[rows, cols] = high
+                to_lo[rows, cols] = low
+
+    def bulk_step(step, _):
+        start = pl.multiple_of(step * FACE, FACE)
+        push_rows(start + FACE, push_hi, push_lo, start, BULK)
         return 0
 
-    lax.fori_loop(0, R // block_rows, push_rows, 0)
-
-    local[6].wait()
+    lax.fori_loop(0, BULK // FACE, bulk_step, 0)
+
+    def coefficients(high, low, chunk):
+        two = dot(high[...], to_modes[chunk])
+        one = dot(low[...], to_modes[chunk, :, 0:LANES])
+        return INV_NU * (two[:, :LANES] + (two[:, LANES:] + one))
+
     backward = {}
-    for off in (2, 1, 3, 0):
+
+    def return_bulk(off):
         to = lax.rem(mi + off, n_modes)
-        two = dot(push_hi[...], to_modes[to])
-        one = dot(push_lo[...], to_modes[to, :, 0:LANES])
-        result = two[:, :LANES] + (two[:, LANES:] + one)
+        result = coefficients(push_hi, push_lo, to)
         for s in range(3):
+            force = result[s * BULK : (s + 1) * BULK] + LAMBDA_COEF * recv[to, s, FACE : FACE + BULK, :]
             if off == 0:
-                back[mi, s] = result[s * R : (s + 1) * R]
+                back[mi, s] = force
             else:
-                sendb[off, s] = result[s * R : (s + 1) * R]
+                sendb[off, s] = force
         if off:
             backward[off] = pltpu.make_async_remote_copy(
-                src_ref=sendb.at[off],
-                dst_ref=back.at[mi],
+                src_ref=sendb.at[off, :, pl.ds(0, MID)],
+                dst_ref=back.at[mi, :, pl.ds(0, MID)],
                 send_sem=bwd_send.at[off],
                 recv_sem=bwd_recv.at[off],
                 device_id=(to, e),
                 device_id_type=MESH,
             )
             backward[off].start()
-    local[7].wait()
+
+    local[8].wait()
+    return_bulk(2)
+    for side, start in enumerate((0, TOP)):
+        push_rows(start, side_hi, side_lo, side * FACE, 2 * FACE)
+    for chunk in range(n_modes):
+        result = coefficients(side_hi, side_lo, chunk)
+        for s in range(3):
+            for side, start in enumerate((0, TOP)):
+                rows = slice((2 * s + side) * FACE, (2 * s + side + 1) * FACE)
+                force = result[rows] + LAMBDA_COEF * recv[chunk, s, start : start + FACE, :]
+                side_out[side, chunk, s] = force
+    side_copies = []
+    for side, who in ((0, below), (1, above)):
+        copy = pltpu.make_async_remote_copy(
+            src_ref=side_out.at[side],
+            dst_ref=side_in.at[1 - side],
+            send_sem=side_sems.at[0, side],
+            recv_sem=side_sems.at[1, 1 - side],
+            device_id=(mi, who),
+            device_id_type=MESH,
+        )
+        copy.start()
+        side_copies.append(copy)
+    for off in (1, 3, 0):
+        return_bulk(off)
+
+    block_row = lax.broadcasted_iota(jnp.int32, (FACE, LANES), 0)
+    met = (
+        jnp.where(block_row < PS, 1.0 - at_low, 0.0),
+        jnp.where((block_row >= 2) & (block_row < 2 + PS), 1.0 - at_high, 0.0),
+    )
+
+    def meet(side, other):
+        return met[side] * pltpu.roll(other, 2 if side else FACE - 2, 0)
+
+    for copy in side_copies:
+        copy.wait_recv()
+    side_returns = []
+    for off in (2, 1, 3, 0):
+        to = lax.rem(mi + off, n_modes)
+        for s in range(3):
+            for side in range(2):
+                total = side_out[side, to, s] + meet(side, side_in[side, to, s])
+                if off == 0:
+                    side_back[mi, s, side] = total
+                else:
+                    side_send[off, s, side] = total
+        if off:
+            copy = pltpu.make_async_remote_copy(
+                src_ref=side_send.at[off],
+                dst_ref=side_back.at[mi],
+                send_sem=fb_send.at[off],
+                recv_sem=fb_recv.at[off],
+                device_id=(to, e),
+                device_id_type=MESH,
+            )
+            copy.start()
+            side_returns.append(copy)
+    local[9].wait()
     for off in (1, 3, 2):
         backward[off].wait_recv()
+    for copy in side_returns:
+        copy.wait_recv()
 
     for g in range(ER):
-        held = slot_ref[0, g]
-        force = [LAMBDA_COEF * slots[held, s] + INV_NU * back[held, s] for s in range(3)]
-        turned = times_unit(force[1])
-        mass = geo[g]
-        img[0, 0, g] = mass * (force[0] + turned)
-        img[0, 1, g] = mass * (force[0] - turned)
-        img[0, 2, g] = mass * force[2]
-
-    face_row = lax.broadcasted_iota(jnp.int32, (ER * PS, 1), 0)
-    inner_high = (lax.rem(face_row, PS) == PS - 1) & (face_row < ER * PS - 1)
-    inner_low = (lax.rem(face_row, PS) == 0) & (face_row > 0)
-
-    def low_rows():
-        return pl.ds(0, PS, stride=PS)
-
-    def high_rows():
-        return pl.ds(PS - 1, PS, stride=PS)
+        pieces = (
+            (slice(0, FACE), [side_back[g, s, 0] for s in range(3)]),
+            (slice(FACE, TOP), [back[g, s, 0:MID, :] for s in range(3)]),
+            (slice(TOP, SENT), [side_back[g, s, 1] for s in range(3)]),
+        )
+        for rows, force in pieces:
+            turned = times_unit(force[1])
+            mass = geo[g, rows, :]
+            img[0, 0, g, rows, :] = mass * (force[0] + turned)
+            img[0, 1, g, rows, :] = mass * (force[0] - turned)
+            img[0, 2, g, rows, :] = mass * force[2]
 
     halos = []
 
     def send_faces(k):
-        for s in range(3):
-            for g in range(ER):
-                rows = slice(g * PS, (g + 1) * PS)
-                face_out[k, 0, s, rows, :] = img[k, s, g, low_rows(), :]
-                face_out[k, 1, s, rows, :] = img[k, s, g, high_rows(), :]
         pairs = []
-        for side_out, who in ((0, below), (1, above)):
+        for side, start, who in ((0, 0, below), (1, TOP, above)):
             copy = pltpu.make_async_remote_copy(
-                src_ref=face_out.at[k, side_out],
-                dst_ref=face_in.at[k, 1 - side_out],
-                send_sem=halo_send.at[k, side_out],
-                recv_sem=halo_recv.at[k, 1 - side_out],
+                src_ref=img.at[k, :, :, pl.ds(start, FACE)],
+                dst_ref=face_in.at[k - 1, 1 - side],
+                send_sem=halo_send.at[k - 1, side],
+                recv_sem=halo_recv.at[k - 1, 1 - side],
                 device_id=(mi, who),
                 device_id_type=MESH,
             )
@@ -436,25 +512,33 @@
             for g in range(ER):
                 vec[k, s, g] = img[k, s, g]
             for g in range(ER - 1):
-                shared = img[k, s, g, NODES - PS : NODES, :] + img[k, s, g + 1, 0:PS, :]
-                vec[k, s, g, NODES - PS : NODES, :] = shared
-                vec[k, s, g + 1, 0:PS, :] = shared
+                last = pl.ds(2 * PS - 1, PS - 2, stride=PS)
+                first = pl.ds(PS, PS - 2, stride=PS)
+                shared = img[k, s, g, last, :] + img[k, s, g + 1, first, :]
+                vec[k, s, g, last, :] = shared
+                vec[k, s, g + 1, first, :] = shared
             for g in range(ER):
-                vec[k, s, g] = vec[k, s, g] * jac[s, g]
+                vec[k, s, g, FACE:TOP, :] = vec[k, s, g, FACE:TOP, :] * jac[s, g, FACE:TOP, :]
 
     def outer_part(k):
-        for copy in halos[k]:
-            copy.wait_recv()
-        for side_in, present, row_set in ((0, 1.0 - at_low, low_rows), (1, 1.0 - at_high, high_rows)):
+        if k > 0:
+            for copy in halos[k - 1]:
+                copy.wait_recv()
+        for side, start, last in ((0, 0, PS - 1), (1, TOP, PS + 1)):
+            rows = slice(start, start + FACE)
             for s in range(3):
-                values = face_in[k, side_in, s]
-                values = values + jnp.where(inner_high, pltpu.roll(values, ER * PS - 1, 0), 0.0)
-                after = face_in[k, side_in, s]
-                values = values + jnp.where(inner_low, pltpu.roll(after, 1, 0), 0.0)
-                values = values * present
+                block = [vec[k, s, g, rows, :] for g in range(ER)]
+                if k > 0:
+                    block = [block[g] + meet(side, face_in[k - 1, side, s, g]) for g in range(ER)]
                 for g in range(ER):
-                    part = values[g * PS : (g + 1) * PS] * jac[s, g, row_set(), :]
-                    vec[k, s, g, row_set(), :] = vec[k, s, g, row_set(), :] + part
+                    total = block[g]
+                    if g + 1 < ER:
+                        nearby = pltpu.roll(block[g + 1], PS - 1, 0)
+                        total = total + jnp.where(block_row == last, nearby, 0.0)
+                    if g > 0:
+                        nearby = pltpu.roll(block[g - 1], FACE - PS + 1, 0)
+                        total = total + jnp.where(block_row == last - PS + 1, nearby, 0.0)
+                    vec[k, s, g, rows, :] = total * jac[s, g, rows, :]
 
     def apply_stiff(k):
         for g in range(ER):
@@ -468,16 +552,19 @@
             for s in range(3):
                 img[k + 1, s, g] = image[:, s * LANES : (s + 1) * LANES]
 
+    share = 1.0 / sharing
+
     def inner(k, left, right):
         for s in range(3):
             total = jnp.zeros((1, LANES), F32)
             for g in range(ER):
                 products = vec[left, s, g] * img[right, s, g]
+                if right == 0:
+                    products = products * share
                 total = total + jnp.sum(products, axis=0, keepdims=True)
             index = k * 3 + s
             moment[index // 9, index % 9 : index % 9 + 1, :] = total
 
-    send_faces(0)
     inner_part(0)
     outer_part(0)
     apply_stiff(0)
@@ -550,10 +637,12 @@
         ]
         results = ((plus + minus) * 0.5, times_unit(minus - plus) * 0.5, axial)
         for s, values in enumerate(results):
-            rows = pl.ds(s * NODES * ER + slot, NODES, stride=ER)
-            out_ref[rows, :] = values[:NODES]
-
-    for copies in (forward.values(), backward.values(), copies_a, copies_b, *halos):
+            for j in range(PS):
+                rows = pl.ds(s * span + j * ER + slot, PS, stride=ER * PS)
+                out_ref[rows, :] = values[j * PS : (j + 1) * PS]
+
+    sent = (forward.values(), backward.values(), side_copies, side_returns, copies_a, copies_b)
+    for copies in (*sent, *halos):
         for copy in copies:
             copy.wait_send()
 
@@ -572,7 +661,7 @@
         scratch_shapes=[
             pltpu.SMEM((1, ER), jnp.int32),
             vmem((1, LANES // 2), jnp.int32),
-            vmem((3 * NODES * ER, LANES), F32),
+            *[vmem((NODES * ER, LANES), F32)] * 3,
             vmem((ER, 3, R, LANES), F32),
             vmem((ER, 3, R, LANES), F32),
             vmem(slopes.shape, BF16),
@@ -583,26 +672,34 @@
             vmem((3 * LANES, 3 * LANES), BF16),
             vmem((6 * R, 3 * LANES), BF16),
             vmem((6 * R, Q), F32),
-            vmem((3 * R, Q), BF16),
-            vmem((3 * R, Q), BF16),
-            vmem((ER, 3, R, LANES), F32),
-            vmem((ER, 3, R, LANES), F32),
+            vmem((3 * BULK, Q), BF16),
+            vmem((3 * BULK, Q), BF16),
+            vmem((6 * FACE, Q), BF16),
+            vmem((6 * FACE, Q), BF16),
+            vmem((ER, 3, BULK, LANES), F32),
+            vmem((ER, 3, BULK, LANES), F32),
+            vmem((2, ER, 3, FACE, LANES), F32),
+            vmem((2, ER, 3, FACE, LANES), F32),
+            vmem((ER, 3, 2, FACE, LANES), F32),
+            vmem((ER, 3, 2, FACE, LANES), F32),
             vmem((3, ER, R, LANES), F32),
             vmem((3, 3, ER, R, LANES), F32),
             vmem((4, 3, ER, R, LANES), F32),
             vmem((ER, 3 * LANES, 3 * LANES), BF16),
-            vmem((3, 2, 3, ER * PS, LANES), F32),
-            vmem((3, 2, 3, ER * PS, LANES), F32),
+            vmem((2, 2, 3, ER, FACE, LANES), F32),
             vmem((2, 16, LANES), F32),
             vmem((ny * nc, 16, LANES), F32),
             vmem((nz, 16, LANES), F32),
-            dma((8,)),
+            dma((10,)),
+            dma((ER, 3)),
+            dma((ER, 3)),
             dma((ER,)),
             dma((ER,)),
+            dma((2, 2)),
             dma((ER,)),
             dma((ER,)),
-            dma((3, 2)),
-            dma((3, 2)),
+            dma((2, 2)),
+            dma((2, 2)),
             dma((ny * nc,)),
             dma((ny * nc,)),
             dma((nz,)),

time: 56.9 us -> 51.9 us (0.912)
  Pallas kernels: 54.8 us -> 49.9 us
    pallas_call x1, Pallas kernels: 54.8 us -> 49.9 us  [on_device(): pl.pallas_call(functools.partial(kernel, grid_shape), out_shape=jax.Shape...]
where the time goes in v3:
time: 51.9 us; the launch traced here: 51.8 us
  Pallas kernels  49.9 us (96%)
  local copies, waits for them, and re-layouts  1.94 us (4%)
    pallas_call x1, Pallas kernels, on_device(): pl.pallas_call(functools.partial(kernel, grid_shape), out_shape=jax.Shape...  49.9 us
    unnamed x1, local copies, waits for them, and re-layouts  1.94 us

profile of v3, /device:TPU:1, one launch (start us, length us, event | category | flops | bytes accessed | tf_op | source)
XLA Modules:
  0.0 51.8 jit_solution(692943759176311181)
XLA Ops:
  0.0 49.9 %shard_map.82 = f32[1200,128]{1,0:T(8,128)} custom-call(s32[1,4]{1,0:T(1,128)} %slot_hbm.1, s32[1,64]{1,0:T(1,128)} %bitcast.9, f32[1200,128]{1,0:T(8,128)} %bitcast.8, bf16[224,384]{1,0:T(8,128)(2,1)} %constant.10.clone.slopes_hbm, bf16[4,112,384]{2,1,0:T(8,128)(2,1)} %constant.11.clone.stiff_hbm, f32[14,112,128]{2,1,0:T(8,128)} %constant.12.clone.geo_hbm, ...), custom_call_target="tpu_custom_call" | custom-call | tf_op jit(solution)/shard_map/pallas_call | solution.py:656
  49.9 1.9 %copy.10 = f32[3,4,10,10,128]{4,1,3,2,0:T(4,128)} copy(f32[3,4,10,10,128]{4,1,3,2,0:T(4,128)} %bitcast.7) | data formatting | bytes 1228800

commit v4 on v3

--- a/solution.py
+++ b/solution.py
@@ -269,20 +269,20 @@
 
     forward = {}
     local[6].wait()
-    for s in range(3):
-        local[s].wait()
-        for off in (2, 1, 3):
-            to = lax.rem(mi + off, n_modes)
-            gather_cell(to, s, cells)
-            forward[off, s] = pltpu.make_async_remote_copy(
-                src_ref=cells.at[to, s, pl.ds(0, SENT)],
-                dst_ref=recv.at[mi, s, pl.ds(0, SENT)],
-                send_sem=fwd_send.at[off, s],
-                recv_sem=fwd_recv.at[off, s],
-                device_id=(to, e),
-                device_id_type=MESH,
-            )
-            forward[off, s].start()
+    for off, s in [(off, s) for off in (1, 3, 2) for s in range(3)]:
+        if off == 1:
+            local[s].wait()
+        to = lax.rem(mi + off, n_modes)
+        gather_cell(to, s, cells)
+        forward[off, s] = pltpu.make_async_remote_copy(
+            src_ref=cells.at[to, s, pl.ds(0, SENT)],
+            dst_ref=recv.at[mi, s, pl.ds(0, SENT)],
+            send_sem=fwd_send.at[off, s],
+            recv_sem=fwd_recv.at[off, s],
+            device_id=(to, e),
+            device_id_type=MESH,
+        )
+        forward[off, s].start()
 
     lane = lax.broadcasted_iota(jnp.int32, (1, LANES), 1)
     even = lax.rem(lane, 2) == 0
@@ -384,7 +384,7 @@
         push_rows(start + FACE, push_hi, push_lo, start, BULK)
         return 0
 
-    lax.fori_loop(0, BULK // FACE, bulk_step, 0)
+    lax.fori_loop(0, BULK // FACE, bulk_step, 0, unroll=True)
 
     def coefficients(high, low, chunk):
         two = dot(high[...], to_modes[chunk])
@@ -655,7 +655,7 @@
     flat = velocity.transpose(0, 2, 3, 1, 4).reshape(3 * NODES * ER, LANES)
     result = pl.pallas_call(
         functools.partial(kernel, grid_shape),
-        out_shape=jax.ShapeDtypeStruct((3 * NODES * ER, LANES), F32),
+        out_shape=vmem((3 * NODES * ER, LANES), F32),
         in_specs=[pl.BlockSpec(memory_space=pltpu.HBM)] * 8,
         out_specs=pl.BlockSpec(memory_space=vmem),
         scratch_shapes=[
@@ -706,17 +706,18 @@
             dma((nz,)),
         ],
         compiler_params=pltpu.CompilerParams(
-            collective_id=0, has_side_effects=True, vmem_limit_bytes=62 * 1024 * 1024
+            collective_id=0, has_side_effects=True, vmem_limit_bytes=48 * 1024 * 1024
         ),
     )(
-        element_slot,
-        lid_noslip.reshape(1, -1),
-        flat,
-        jnp.asarray(slopes),
-        jnp.asarray(stiff),
-        jnp.asarray(geometry),
-        jnp.asarray(to_planes),
-        jnp.asarray(to_modes),
+        *[
+            pltpu.with_memory_space_constraint(operand, pltpu.HBM)
+            for operand in (
+                element_slot,
+                lid_noslip.reshape(1, -1),
+                flat,
+                *[jnp.asarray(table) for table in (slopes, stiff, geometry, to_planes, to_modes)],
+            )
+        ]
     )
     return result.reshape(3, PS, PS, ER, LANES).transpose(0, 3, 1, 2, 4)
 

time: 51.9 us -> 48.4 us (0.933)
  Pallas kernels: 49.9 us -> 47.5 us
  local copies, waits for them, and re-layouts: 1.94 us -> 0.83 us
    pallas_call x1, Pallas kernels: 49.9 us -> 47.5 us  [on_device(): pl.pallas_call(functools.partial(kernel, grid_shape), out_shape=vmem((3 *...]
    unnamed x1, local copies, waits for them, and re-layouts: 1.94 us -> 0.83 us
where the time goes in v4:
time: 48.4 us; the launch traced here: 48.3 us
  Pallas kernels  47.5 us (98%)
  local copies, waits for them, and re-layouts  0.83 us (2%)
    pallas_call x1, Pallas kernels, on_device(): pl.pallas_call(functools.partial(kernel, grid_shape), out_shape=vmem((3 *...  47.5 us

profile of v4, /device:TPU:1, one launch (start us, length us, event | category | flops | bytes accessed | tf_op | source)
XLA Modules:
  0.0 48.3 jit_solution(11938827867135782954)
XLA Ops:
  0.0 47.5 %shard_map.82 = f32[1200,128]{1,0:T(8,128)S(1)} custom-call(s32[1,4]{1,0:T(1,128)} %slot_hbm.1, s32[1,64]{1,0:T(1,128)} %bitcast.9, f32[1200,128]{1,0:T(8,128)} %bitcast.8, bf16[224,384]{1,0:T(8,128)(2,1)} %constant.10.clone.slopes_hbm, bf16[4,112,384]{2,1,0:T(8,128)(2,1)} %constant.11.clone.stiff_hbm, f32[14,112,128]{2,1,0:T(8,128)} %constant.12.clone.geo_hbm, ...), custom_call_target="tpu_custom_call" | custom-call | tf_op jit(solution)/shard_map/pallas_call | solution.py:656
  47.5 0.8 %copy.10 = f32[3,4,10,10,128]{4,1,3,2,0:T(4,128)} copy(f32[3,4,10,10,128]{4,1,3,2,0:T(4,128)S(1)} %bitcast.7) | data formatting | bytes 1228800

commit v5 on v4

--- a/solution.py
+++ b/solution.py
@@ -12,10 +12,12 @@
 PS = 10
 NODES = PS * PS
 R = 112
-SENT = 104
 TOP = 88
 FACE = 16
+FACE_AT = (0, NODES - PS - TOP)
 MID = TOP - FACE
+ENDS = NODES - MID
+MOMENTS = 9
 BULK = 80
 M = 256
 Q = 768
@@ -242,9 +244,9 @@
 
     for g in range(ER):
         for s in range(3):
-            cells[g, s, R - 16 :, :] = jnp.zeros((16, LANES), F32)
             recv[g, s, R - 16 :, :] = jnp.zeros((16, LANES), F32)
-            img[0, s, g, SENT:, :] = jnp.zeros((R - SENT, LANES), F32)
+            img[0, s, g, TOP + FACE :, :] = jnp.zeros((R - TOP - FACE, LANES), F32)
+            side_back[g, s, 2 * FACE - 8 :, :] = jnp.zeros((8, LANES), F32)
     no_rows = jnp.zeros((LANES - R, 3 * LANES), BF16)
     for part in range(3):
         rhs[part * LANES + R : (part + 1) * LANES, :] = no_rows
@@ -275,8 +277,8 @@
         to = lax.rem(mi + off, n_modes)
         gather_cell(to, s, cells)
         forward[off, s] = pltpu.make_async_remote_copy(
-            src_ref=cells.at[to, s, pl.ds(0, SENT)],
-            dst_ref=recv.at[mi, s, pl.ds(0, SENT)],
+            src_ref=cells.at[to, s, pl.ds(0, NODES)],
+            dst_ref=recv.at[mi, s, pl.ds(0, NODES)],
             send_sem=fwd_send.at[off, s],
             recv_sem=fwd_recv.at[off, s],
             device_id=(to, e),
@@ -427,8 +429,8 @@
     side_copies = []
     for side, who in ((0, below), (1, above)):
         copy = pltpu.make_async_remote_copy(
-            src_ref=side_out.at[side],
-            dst_ref=side_in.at[1 - side],
+            src_ref=side_out.at[side, :, :, pl.ds(FACE_AT[side], PS)],
+            dst_ref=side_in.at[1 - side, :, :, pl.ds(FACE_AT[1 - side], PS)],
             send_sem=side_sems.at[0, side],
             recv_sem=side_sems.at[1, 1 - side],
             device_id=(mi, who),
@@ -441,12 +443,12 @@
 
     block_row = lax.broadcasted_iota(jnp.int32, (FACE, LANES), 0)
     met = (
-        jnp.where(block_row < PS, 1.0 - at_low, 0.0),
-        jnp.where((block_row >= 2) & (block_row < 2 + PS), 1.0 - at_high, 0.0),
+        (block_row < PS) & (e > 0),
+        (block_row >= FACE_AT[1]) & (block_row < FACE_AT[1] + PS) & (e < n_elem - 1),
     )
 
     def meet(side, other):
-        return met[side] * pltpu.roll(other, 2 if side else FACE - 2, 0)
+        return jnp.where(met[side], other, 0.0)
 
     for copy in side_copies:
         copy.wait_recv()
@@ -456,14 +458,15 @@
         for s in range(3):
             for side in range(2):
                 total = side_out[side, to, s] + meet(side, side_in[side, to, s])
+                rows = slice(side * FACE, (side + 1) * FACE)
                 if off == 0:
-                    side_back[mi, s, side] = total
+                    side_back[mi, s, rows, :] = total
                 else:
-                    side_send[off, s, side] = total
+                    side_send[off, s, rows, :] = total
         if off:
             copy = pltpu.make_async_remote_copy(
-                src_ref=side_send.at[off],
-                dst_ref=side_back.at[mi],
+                src_ref=side_send.at[off, :, pl.ds(0, ENDS)],
+                dst_ref=side_back.at[mi, :, pl.ds(0, ENDS)],
                 send_sem=fb_send.at[off],
                 recv_sem=fb_recv.at[off],
                 device_id=(to, e),
@@ -479,9 +482,9 @@
 
     for g in range(ER):
         pieces = (
-            (slice(0, FACE), [side_back[g, s, 0] for s in range(3)]),
+            (slice(0, FACE), [side_back[g, s, 0:FACE, :] for s in range(3)]),
             (slice(FACE, TOP), [back[g, s, 0:MID, :] for s in range(3)]),
-            (slice(TOP, SENT), [side_back[g, s, 1] for s in range(3)]),
+            (slice(TOP, TOP + FACE), [side_back[g, s, FACE:, :] for s in range(3)]),
         )
         for rows, force in pieces:
             turned = times_unit(force[1])
@@ -494,10 +497,10 @@
 
     def send_faces(k):
         pairs = []
-        for side, start, who in ((0, 0, below), (1, TOP, above)):
+        for side, start, who in ((0, 0, below), (1, NODES - PS, above)):
             copy = pltpu.make_async_remote_copy(
-                src_ref=img.at[k, :, :, pl.ds(start, FACE)],
-                dst_ref=face_in.at[k - 1, 1 - side],
+                src_ref=img.at[k, :, :, pl.ds(start, PS)],
+                dst_ref=face_in.at[k - 1, 1 - side, :, :, pl.ds(FACE_AT[1 - side], PS)],
                 send_sem=halo_send.at[k - 1, side],
                 recv_sem=halo_recv.at[k - 1, 1 - side],
                 device_id=(mi, who),
@@ -563,7 +566,8 @@
                     products = products * share
                 total = total + jnp.sum(products, axis=0, keepdims=True)
             index = k * 3 + s
-            moment[index // 9, index % 9 : index % 9 + 1, :] = total
+            at = index % MOMENTS
+            moment[index // MOMENTS, at : at + 1, :] = total
 
     inner_part(0)
     outer_part(0)
@@ -587,8 +591,8 @@
         copies = []
         for off in range(1, size):
             copy = pltpu.make_async_remote_copy(
-                src_ref=buffer.at[rank],
-                dst_ref=buffer.at[rank],
+                src_ref=buffer.at[rank, pl.ds(0, MOMENTS)],
+                dst_ref=buffer.at[rank, pl.ds(0, MOMENTS)],
                 send_sem=send_sems.at[off],
                 recv_sem=recv_sems.at[off],
                 device_id=(mi, member(lax.rem(rank + off, size))),
@@ -598,14 +602,14 @@
             copies.append(copy)
         for copy in copies:
             copy.wait_recv()
-        total = buffer[0]
+        total = buffer[0, 0:MOMENTS, :]
         for t in range(1, size):
-            total = total + buffer[t]
+            total = total + buffer[t, 0:MOMENTS, :]
         return total, copies
 
     red_a[rank_a] = jnp.where(even, pair_sum(moment[0]), pair_sum(moment[1]))
     total, copies_a = exchange(red_a, rank_a, size_a, member_a, a_send, a_recv)
-    red_b[zc] = total
+    red_b[zc, 0:MOMENTS, :] = total
     total, copies_b = exchange(red_b, zc, nz, member_b, b_send, b_recv)
     first = jnp.where(even, total, pltpu.roll(total, 1, 1))
     second = jnp.where(even, pltpu.roll(total, LANES - 1, 1), total)
@@ -680,8 +684,8 @@
             vmem((ER, 3, BULK, LANES), F32),
             vmem((2, ER, 3, FACE, LANES), F32),
             vmem((2, ER, 3, FACE, LANES), F32),
-            vmem((ER, 3, 2, FACE, LANES), F32),
-            vmem((ER, 3, 2, FACE, LANES), F32),
+            vmem((ER, 3, 2 * FACE, LANES), F32),
+            vmem((ER, 3, 2 * FACE, LANES), F32),
             vmem((3, ER, R, LANES), F32),
             vmem((3, 3, ER, R, LANES), F32),
             vmem((4, 3, ER, R, LANES), F32),

time: 48.4 us -> 46.4 us (0.959)
  Pallas kernels: 47.5 us -> 45.5 us
    pallas_call x1, Pallas kernels: 47.5 us -> 45.5 us  [on_device(): pl.pallas_call(functools.partial(kernel, grid_shape), out_shape=vmem((3 *...]
where the time goes in v5:
time: 46.4 us
  Pallas kernels  45.5 us (98%)
  local copies, waits for them, and re-layouts  0.83 us (2%)
    pallas_call x1, Pallas kernels, on_device(): pl.pallas_call(functools.partial(kernel, grid_shape), out_shape=vmem((3 *...  45.5 us

profile of v5, /device:TPU:1, one launch (start us, length us, event | category | flops | bytes accessed | tf_op | source)
XLA Modules:
  0.0 46.4 jit_solution(2761935468266016029)
XLA Ops:
  0.0 45.5 %shard_map.82 = f32[1200,128]{1,0:T(8,128)S(1)} custom-call(s32[1,4]{1,0:T(1,128)} %slot_hbm.1, s32[1,64]{1,0:T(1,128)} %bitcast.9, f32[1200,128]{1,0:T(8,128)} %bitcast.8, bf16[224,384]{1,0:T(8,128)(2,1)} %constant.10.clone.slopes_hbm, bf16[4,112,384]{2,1,0:T(8,128)(2,1)} %constant.11.clone.stiff_hbm, f32[14,112,128]{2,1,0:T(8,128)} %constant.12.clone.geo_hbm, ...), custom_call_target="tpu_custom_call" | custom-call | tf_op jit(solution)/shard_map/pallas_call | solution.py:660
  45.5 0.8 %copy.10 = f32[3,4,10,10,128]{4,1,3,2,0:T(4,128)} copy(f32[3,4,10,10,128]{4,1,3,2,0:T(4,128)S(1)} %bitcast.7) | data formatting | bytes 1228800

commit v6 on v5

--- a/solution.py
+++ b/solution.py
@@ -181,6 +181,7 @@
     jac,
     vec,
     img,
+    ordered,
     krhs,
     face_in,
     moment,
@@ -306,34 +307,45 @@
     inv_radius = 1.0 / radius
     swirl_base = SWIRL_SLOPE * radius + SWIRL_CURVE * inv_radius
 
-    def add_modes(block, source, first):
-        for s in range(3):
+    def slope_of(block, comps, rows):
+        for s in comps:
             high, low = split(block[s])
             cols = slice(s * LANES, (s + 1) * LANES)
             rhs[0:R, cols] = high
             rhs[LANES : LANES + R, cols] = low
             rhs[2 * LANES : 2 * LANES + R, cols] = high
-        slope = dot(slopes[...], rhs[...])
-        d_r = [slope[:R, s * LANES : (s + 1) * LANES] for s in range(3)]
-        d_z = [slope[R:, s * LANES : (s + 1) * LANES] for s in range(3)]
-        wave = pair + (source * (LANES // 2)).astype(F32)
-        u_r, u_t, u_z = block[0], block[1], block[2]
-        curl_r = wave * times_unit(u_z) * inv_radius - d_z[1]
-        curl_t = d_z[0] - d_r[2]
-        curl_z = d_r[1] + (u_t - wave * times_unit(u_r)) * inv_radius
-        for f, values in enumerate((u_r, u_t, u_z, curl_r, curl_t, curl_z)):
-            high, low = split(values)
-            rows = slice(f * R, (f + 1) * R)
+        return dot(slopes[0:rows, :], rhs[:, comps[0] * LANES : (comps[-1] + 1) * LANES])
+
+    def add_fields(values, source, half, first):
+        for f, field in enumerate(values):
+            high, low = split(field)
+            rows = slice((3 * half + f) * R, (3 * half + f + 1) * R)
             fields[rows, 0:LANES] = high
             fields[rows, LANES : 2 * LANES] = low
             fields[rows, 2 * LANES :] = high
-        terms = dot(fields[...], to_planes[source])
+        rows = slice(3 * half * R, 3 * (half + 1) * R)
+        terms = dot(fields[rows, :], to_planes[source])
         if first:
-            planes[...] = terms
+            planes[rows, :] = terms
         else:
-            planes[...] += terms
-
-    add_modes(recv.at[mi], mi, True)
+            planes[rows, :] += terms
+
+    def add_modes(block, source, first, arrived):
+        wave = pair + (source * (LANES // 2)).astype(F32)
+        arrived(0)
+        arrived(1)
+        slope = slope_of(block, (0, 1), 2 * R)
+        u_r, u_t = block[0], block[1]
+        d_z = [slope[R:, s * LANES : (s + 1) * LANES] for s in range(2)]
+        curl_z = slope[:R, LANES:] + (u_t - wave * times_unit(u_r)) * inv_radius
+        add_fields((u_r, u_t, curl_z), source, 0, first)
+        arrived(2)
+        slope = slope_of(block, (2,), R)
+        u_z = block[2]
+        curl_r = wave * times_unit(u_z) * inv_radius - d_z[1]
+        add_fields((u_z, curl_r, d_z[0] - slope), source, 1, first)
+
+    add_modes(recv.at[mi], mi, True, lambda s: None)
 
     lid = lid_ref[...].astype(BF16)
     wide = lax.broadcasted_iota(jnp.int32, (LANES // 2, LANES), 1) // 2
@@ -354,10 +366,8 @@
             jac[s, g] = jnp.where(fixed > 0.0, lid_keep / jnp.where(fixed > 0.0, diag, 1.0), 0.0)
 
     for off in (1, 3, 2):
-        for s in range(3):
-            forward[off, s].wait_recv()
         source = lax.rem(mi + n_modes - off, n_modes)
-        add_modes(recv.at[source], source, False)
+        add_modes(recv.at[source], source, False, lambda s: forward[off, s].wait_recv())
 
     def push_rows(start, to_hi, to_lo, first, pitch):
         def field(f, cols):
@@ -368,7 +378,7 @@
         swirl = jnp.concatenate([swirl] * 3, axis=1)
         spin = 2.0 * SWIRL_SLOPE
         for cols in (slice(0, 3 * LANES), slice(3 * LANES, 6 * LANES)):
-            u_r, u_t, u_z, w_r, w_t, w_z = [field(f, cols) for f in range(6)]
+            u_r, u_t, w_z, u_z, w_r, w_t = [field(f, cols) for f in range(6)]
             turned = u_t + swirl
             results = (
                 turned * w_z - u_z * w_t + spin * u_t,
@@ -522,6 +532,7 @@
                 vec[k, s, g + 1, first, :] = shared
             for g in range(ER):
                 vec[k, s, g, FACE:TOP, :] = vec[k, s, g, FACE:TOP, :] * jac[s, g, FACE:TOP, :]
+                split_rows(k, g, s, FACE, BULK)
 
     def outer_part(k):
         if k > 0:
@@ -543,14 +554,18 @@
                         total = total + jnp.where(block_row == last - PS + 1, nearby, 0.0)
                     vec[k, s, g, rows, :] = total * jac[s, g, rows, :]
 
+    def split_rows(k, g, s, start, stop):
+        high, low = split(vec[k, s, g, start:stop, :])
+        cols = slice(s * LANES, (s + 1) * LANES)
+        krhs[g, start:stop, cols] = high
+        krhs[g, LANES + start : LANES + stop, cols] = low
+        krhs[g, 2 * LANES + start : 2 * LANES + stop, cols] = high
+
     def apply_stiff(k):
         for g in range(ER):
             for s in range(3):
-                high, low = split(vec[k, s, g])
-                cols = slice(s * LANES, (s + 1) * LANES)
-                krhs[g, 0:R, cols] = high
-                krhs[g, LANES : LANES + R, cols] = low
-                krhs[g, 2 * LANES : 2 * LANES + R, cols] = high
+                split_rows(k, g, s, 0, FACE)
+                split_rows(k, g, s, BULK, R)
             image = dot(stiff[g], krhs[g])
             for s in range(3):
                 img[k + 1, s, g] = image[:, s * LANES : (s + 1) * LANES]
@@ -559,12 +574,12 @@
 
     def inner(k, left, right):
         for s in range(3):
-            total = jnp.zeros((1, LANES), F32)
-            for g in range(ER):
-                products = vec[left, s, g] * img[right, s, g]
-                if right == 0:
-                    products = products * share
-                total = total + jnp.sum(products, axis=0, keepdims=True)
+            products = vec[left, s, 0] * img[right, s, 0]
+            for g in range(1, ER):
+                products = products + vec[left, s, g] * img[right, s, g]
+            if right == 0:
+                products = products * share
+            total = jnp.sum(products, axis=0, keepdims=True)
             index = k * 3 + s
             at = index % MOMENTS
             moment[index // MOMENTS, at : at + 1, :] = total
@@ -587,7 +602,18 @@
     inner(4, 2, 2)
     inner(5, 2, 3)
 
-    def exchange(buffer, rank, size, member, send_sems, recv_sems):
+    def arrange():
+        for slot in range(ER):
+            held = jnp.int32(0)
+            for g in range(ER):
+                held = jnp.where(slot_ref[0, g] == slot, g, held)
+            for k in range(3):
+                for s in range(3):
+                    for j in range(PS):
+                        rows = pl.ds(j * ER + slot, PS, stride=ER * PS)
+                        ordered[k, s, rows, :] = vec[k, s, held, j * PS : (j + 1) * PS, :]
+
+    def exchange(buffer, rank, size, member, send_sems, recv_sems, meanwhile):
         copies = []
         for off in range(1, size):
             copy = pltpu.make_async_remote_copy(
@@ -600,6 +626,7 @@
             )
             copy.start()
             copies.append(copy)
+        meanwhile()
         for copy in copies:
             copy.wait_recv()
         total = buffer[0, 0:MOMENTS, :]
@@ -608,9 +635,9 @@
         return total, copies
 
     red_a[rank_a] = jnp.where(even, pair_sum(moment[0]), pair_sum(moment[1]))
-    total, copies_a = exchange(red_a, rank_a, size_a, member_a, a_send, a_recv)
+    total, copies_a = exchange(red_a, rank_a, size_a, member_a, a_send, a_recv, arrange)
     red_b[zc, 0:MOMENTS, :] = total
-    total, copies_b = exchange(red_b, zc, nz, member_b, b_send, b_recv)
+    total, copies_b = exchange(red_b, zc, nz, member_b, b_send, b_recv, lambda: None)
     first = jnp.where(even, total, pltpu.roll(total, 1, 1))
     second = jnp.where(even, pltpu.roll(total, LANES - 1, 1), total)
 
@@ -631,19 +658,18 @@
         c0 = h[0] / g00 - ratio1 * c1 - ratio2 * c2
         coefs.append((c0, c1, c2))
 
-    for slot in range(ER):
-        held = jnp.int32(0)
-        for g in range(ER):
-            held = jnp.where(slot_ref[0, g] == slot, g, held)
+    block = 2 * ER * PS
+    for start in range(0, span, block):
+        rows = slice(start, start + block)
         plus, minus, axial = [
-            coefs[s][0] * vec[0, s, held] + coefs[s][1] * vec[1, s, held] + coefs[s][2] * vec[2, s, held]
+            coefs[s][0] * ordered[0, s, rows, :]
+            + coefs[s][1] * ordered[1, s, rows, :]
+            + coefs[s][2] * ordered[2, s, rows, :]
             for s in range(3)
         ]
         results = ((plus + minus) * 0.5, times_unit(minus - plus) * 0.5, axial)
         for s, values in enumerate(results):
-            for j in range(PS):
-                rows = pl.ds(s * span + j * ER + slot, PS, stride=ER * PS)
-                out_ref[rows, :] = values[j * PS : (j + 1) * PS]
+            out_ref[s * span + start : s * span + start + block, :] = values
 
     sent = (forward.values(), backward.values(), side_copies, side_returns, copies_a, copies_b)
     for copies in (*sent, *halos):
@@ -689,6 +715,7 @@
             vmem((3, ER, R, LANES), F32),
             vmem((3, 3, ER, R, LANES), F32),
             vmem((4, 3, ER, R, LANES), F32),
+            vmem((3, 3, NODES * ER, LANES), F32),
             vmem((ER, 3 * LANES, 3 * LANES), BF16),
             vmem((2, 2, 3, ER, FACE, LANES), F32),
             vmem((2, 16, LANES), F32),

time: 46.4 us -> 46 us (level)
  no operation moved by 1% of the time
where the time goes in v6:
time: 46 us; the launch traced here: 45.9 us
  Pallas kernels  45.1 us (98%)
  local copies, waits for them, and re-layouts  0.83 us (2%)
    pallas_call x1, Pallas kernels, on_device(): pl.pallas_call(functools.partial(kernel, grid_shape), out_shape=vmem((3 *...  45.1 us

profile of v6, /device:TPU:1, one launch (start us, length us, event | category | flops | bytes accessed | tf_op | source)
XLA Modules:
  0.0 45.9 jit_solution(1602333193144456927)
XLA Ops:
  0.0 45.1 %shard_map.82 = f32[1200,128]{1,0:T(8,128)S(1)} custom-call(s32[1,4]{1,0:T(1,128)} %slot_hbm.1, s32[1,64]{1,0:T(1,128)} %bitcast.9, f32[1200,128]{1,0:T(8,128)} %bitcast.8, bf16[224,384]{1,0:T(8,128)(2,1)} %constant.10.clone.slopes_hbm, bf16[4,112,384]{2,1,0:T(8,128)(2,1)} %constant.11.clone.stiff_hbm, f32[14,112,128]{2,1,0:T(8,128)} %constant.12.clone.geo_hbm, ...), custom_call_target="tpu_custom_call" | custom-call | tf_op jit(solution)/shard_map/pallas_call | solution.py:686
  45.1 0.8 %copy.10 = f32[3,4,10,10,128]{4,1,3,2,0:T(4,128)} copy(f32[3,4,10,10,128]{4,1,3,2,0:T(4,128)S(1)} %bitcast.7) | data formatting | bytes 1228800

commit v7 on v6

--- a/solution.py
+++ b/solution.py
@@ -152,7 +152,8 @@
     geo_hbm,
     planes_hbm,
     modes_hbm,
-    out_ref,
+    ordered,
+    total_ref,
     slot_ref,
     lid_ref,
     vel_r,
@@ -181,7 +182,6 @@
     jac,
     vec,
     img,
-    ordered,
     krhs,
     face_in,
     moment,
@@ -222,6 +222,14 @@
     above = lax.rem(e + 1, n_elem)
     below = lax.rem(e + n_elem - 1, n_elem)
 
+    barrier = pltpu.get_barrier_semaphore()
+    greeted = [(lax.rem(mi + t, n_modes), e) for t in range(1, n_modes)]
+    greeted += [(mi, above), (mi, below)]
+    greeted += [(mi, member_a(lax.rem(rank_a + t, size_a))) for t in range(1, size_a)]
+    greeted += [(mi, member_b(lax.rem(zc + t, nz))) for t in range(1, nz)]
+    for who in greeted:
+        pl.semaphore_signal(barrier, inc=1, device_id=who, device_id_type=MESH)
+
     span = NODES * ER
     vel = (vel_r, vel_t, vel_z)
     local_pairs = [
@@ -240,12 +248,12 @@
     local = [
         pltpu.make_async_copy(src, dst, local_sem.at[i]) for i, (src, dst) in enumerate(local_pairs)
     ]
-    for copy in local:
-        copy.start()
+    for i in (6, 0, 1, 2, 3, 4, 5, 7, 8, 9):
+        local[i].start()
 
     for g in range(ER):
         for s in range(3):
-            recv[g, s, R - 16 :, :] = jnp.zeros((16, LANES), F32)
+            recv[g, s, NODES:, :] = jnp.zeros((R - NODES, LANES), F32)
             img[0, s, g, TOP + FACE :, :] = jnp.zeros((R - TOP - FACE, LANES), F32)
             side_back[g, s, 2 * FACE - 8 :, :] = jnp.zeros((8, LANES), F32)
     no_rows = jnp.zeros((LANES - R, 3 * LANES), BF16)
@@ -261,22 +269,19 @@
             rows = pl.ds(j * ER + held, PS, stride=ER * PS)
             target[g, s, j * PS : (j + 1) * PS, :] = vel[s][rows, :]
 
-    barrier = pltpu.get_barrier_semaphore()
-    greeted = [(lax.rem(mi + t, n_modes), e) for t in range(1, n_modes)]
-    greeted += [(mi, above), (mi, below)]
-    greeted += [(mi, member_a(lax.rem(rank_a + t, size_a))) for t in range(1, size_a)]
-    greeted += [(mi, member_b(lax.rem(zc + t, nz))) for t in range(1, nz)]
-    for who in greeted:
-        pl.semaphore_signal(barrier, inc=1, device_id=who, device_id_type=MESH)
+    local[6].wait()
+    local[0].wait()
+    for off in (1, 3, 2):
+        gather_cell(lax.rem(mi + off, n_modes), 0, cells)
     pl.semaphore_wait(barrier, len(greeted))
 
     forward = {}
-    local[6].wait()
     for off, s in [(off, s) for off in (1, 3, 2) for s in range(3)]:
-        if off == 1:
+        if off == 1 and s > 0:
             local[s].wait()
         to = lax.rem(mi + off, n_modes)
-        gather_cell(to, s, cells)
+        if s > 0:
+            gather_cell(to, s, cells)
         forward[off, s] = pltpu.make_async_remote_copy(
             src_ref=cells.at[to, s, pl.ds(0, NODES)],
             dst_ref=recv.at[mi, s, pl.ds(0, NODES)],
@@ -638,6 +643,23 @@
     total, copies_a = exchange(red_a, rank_a, size_a, member_a, a_send, a_recv, arrange)
     red_b[zc, 0:MOMENTS, :] = total
     total, copies_b = exchange(red_b, zc, nz, member_b, b_send, b_recv, lambda: None)
+    total_ref[...] = total
+
+    sent = (forward.values(), backward.values(), side_copies, side_returns, copies_a, copies_b)
+    for copies in (*sent, *halos):
+        for copy in copies:
+            copy.wait_send()
+
+
+def combine(ordered, total_ref, out_hbm, out_ref, sems):
+    span = NODES * ER
+    lane = lax.broadcasted_iota(jnp.int32, (1, LANES), 1)
+    even = lax.rem(lane, 2) == 0
+
+    def times_unit(values):
+        return jnp.where(even, -pltpu.roll(values, LANES - 1, 1), pltpu.roll(values, 1, 1))
+
+    total = total_ref[...]
     first = jnp.where(even, total, pltpu.roll(total, 1, 1))
     second = jnp.where(even, pltpu.roll(total, LANES - 1, 1), total)
 
@@ -659,6 +681,7 @@
         coefs.append((c0, c1, c2))
 
     block = 2 * ER * PS
+    copies = []
     for start in range(0, span, block):
         rows = slice(start, start + block)
         plus, minus, axial = [
@@ -670,11 +693,15 @@
         results = ((plus + minus) * 0.5, times_unit(minus - plus) * 0.5, axial)
         for s, values in enumerate(results):
             out_ref[s * span + start : s * span + start + block, :] = values
-
-    sent = (forward.values(), backward.values(), side_copies, side_returns, copies_a, copies_b)
-    for copies in (*sent, *halos):
-        for copy in copies:
-            copy.wait_send()
+            rows = pl.ds(s * span + start, block)
+            copy = pltpu.make_async_copy(
+                out_ref.at[rows], out_hbm.at[rows], sems.at[s, start // block]
+            )
+            copy.start()
+            copies.append(copy)
+
+    for copy in copies:
+        copy.wait()
 
 
 def on_device(grid_shape, velocity, element_slot, lid_noslip):
@@ -683,11 +710,11 @@
     vmem = pltpu.VMEM
     dma = pltpu.SemaphoreType.DMA
     flat = velocity.transpose(0, 2, 3, 1, 4).reshape(3 * NODES * ER, LANES)
-    result = pl.pallas_call(
+    ordered, total = pl.pallas_call(
         functools.partial(kernel, grid_shape),
-        out_shape=vmem((3 * NODES * ER, LANES), F32),
+        out_shape=(vmem((3, 3, NODES * ER, LANES), F32), vmem((MOMENTS, LANES), F32)),
         in_specs=[pl.BlockSpec(memory_space=pltpu.HBM)] * 8,
-        out_specs=pl.BlockSpec(memory_space=vmem),
+        out_specs=(pl.BlockSpec(memory_space=vmem),) * 2,
         scratch_shapes=[
             pltpu.SMEM((1, ER), jnp.int32),
             vmem((1, LANES // 2), jnp.int32),
@@ -715,7 +742,6 @@
             vmem((3, ER, R, LANES), F32),
             vmem((3, 3, ER, R, LANES), F32),
             vmem((4, 3, ER, R, LANES), F32),
-            vmem((3, 3, NODES * ER, LANES), F32),
             vmem((ER, 3 * LANES, 3 * LANES), BF16),
             vmem((2, 2, 3, ER, FACE, LANES), F32),
             vmem((2, 16, LANES), F32),
@@ -750,6 +776,13 @@
             )
         ]
     )
+    result = pl.pallas_call(
+        combine,
+        out_shape=jax.ShapeDtypeStruct((3 * NODES * ER, LANES), F32),
+        in_specs=[pl.BlockSpec(memory_space=vmem)] * 2,
+        out_specs=pl.BlockSpec(memory_space=pl.ANY),
+        scratch_shapes=[vmem((3 * NODES * ER, LANES), F32), dma((3, 5))],
+    )(*[pltpu.with_memory_space_constraint(held, pltpu.VMEM) for held in (ordered, total)])
     return result.reshape(3, PS, PS, ER, LANES).transpose(0, 3, 1, 2, 4)
 
 

time: 46 us -> 45.8 us (level)
  local copies, waits for them, and re-layouts: 0.83 us -> 0 us
  Pallas kernels: 45.1 us -> 45.7 us
    unnamed x1 -> x0, local copies, waits for them, and re-layouts: 0.83 us -> none
    pallas_call x1 -> x2, Pallas kernels: 45.1 us -> 45.7 us  [the longest x1 44.6 us: on_device(): pl.pallas_call(functools.partial(kernel, grid_shape), out_shape=(vmem((3,...]
where the time goes in v7:
time: 45.8 us; the launch traced here: 45.7 us
  Pallas kernels  45.7 us (100%)
    pallas_call x1, Pallas kernels, on_device(): pl.pallas_call(functools.partial(kernel, grid_shape), out_shape=(vmem((3,...  44.6 us
    pallas_call x1, Pallas kernels, on_device(): pl.pallas_call(combine, out_shape=jax.ShapeDtypeStruct((3 * NODES * ER, L...  1.13 us

profile of v7, /device:TPU:1, one launch (start us, length us, event | category | flops | bytes accessed | tf_op | source)
XLA Modules:
  0.0 45.7 jit_solution(6894735200879329802)
XLA Ops:
  0.0 44.6 %shard_map.82 = (f32[3,3,400,128]{3,2,1,0:T(8,128)S(1)}, f32[9,128]{1,0:T(8,128)S(1)}) custom-call(s32[1,4]{1,0:T(1,128)} %slot_hbm.1, s32[1,64]{1,0:T(1,128)} %bitcast.8, f32[1200,128]{1,0:T(8,128)} %bitcast.7, bf16[224,384]{1,0:T(8,128)(2,1)} %constant.10.clone.slopes_hbm, bf16[4,112,384]{2,1,0:T(8,128)(2,1)} %constant.11.clone.stiff_hbm, ...), custom_call_target="tpu_custom_call" | custom-call | tf_op jit(solution)/shard_map/pallas_call | solution.py:713
  44.6 1.1 %shard_map.83 = f32[1200,128]{1,0:T(8,128)} custom-call(f32[3,3,400,128]{3,2,1,0:T(8,128)S(1)} %get-tuple-element.7.ordered, f32[9,128]{1,0:T(8,128)S(1)} %get-tuple-element.8.total_ref), custom_call_target="tpu_custom_call" | custom-call | tf_op jit(solution)/shard_map/pallas_call | solution.py:779

commit v8 on v7

--- a/solution.py
+++ b/solution.py
@@ -276,7 +276,7 @@
     pl.semaphore_wait(barrier, len(greeted))
 
     forward = {}
-    for off, s in [(off, s) for off in (1, 3, 2) for s in range(3)]:
+    for off, s in [(off, s) for group in ((1, 3), (2,)) for s in range(3) for off in group]:
         if off == 1 and s > 0:
             local[s].wait()
         to = lax.rem(mi + off, n_modes)

time: 45.8 us -> 45.8 us (level)
  no operation moved by 1% of the time
where the time goes in v8:
time: 45.8 us; the launch traced here: 45.7 us
  Pallas kernels  45.7 us (100%)
    pallas_call x1, Pallas kernels, on_device(): pl.pallas_call(functools.partial(kernel, grid_shape), out_shape=(vmem((3,...  44.6 us
    pallas_call x1, Pallas kernels, on_device(): pl.pallas_call(combine, out_shape=jax.ShapeDtypeStruct((3 * NODES * ER, L...  1.13 us

profile of v8, /device:TPU:1, one launch (start us, length us, event | category | flops | bytes accessed | tf_op | source)
XLA Modules:
  0.0 45.7 jit_solution(16711292384820276690)
XLA Ops:
  0.0 44.6 %shard_map.82 = (f32[3,3,400,128]{3,2,1,0:T(8,128)S(1)}, f32[9,128]{1,0:T(8,128)S(1)}) custom-call(s32[1,4]{1,0:T(1,128)} %slot_hbm.1, s32[1,64]{1,0:T(1,128)} %bitcast.8, f32[1200,128]{1,0:T(8,128)} %bitcast.7, bf16[224,384]{1,0:T(8,128)(2,1)} %constant.10.clone.slopes_hbm, bf16[4,112,384]{2,1,0:T(8,128)(2,1)} %constant.11.clone.stiff_hbm, ...), custom_call_target="tpu_custom_call" | custom-call | tf_op jit(solution)/shard_map/pallas_call | solution.py:713
  44.6 1.1 %shard_map.83 = f32[1200,128]{1,0:T(8,128)} custom-call(f32[3,3,400,128]{3,2,1,0:T(8,128)S(1)} %get-tuple-element.7.ordered, f32[9,128]{1,0:T(8,128)S(1)} %get-tuple-element.8.total_ref), custom_call_target="tpu_custom_call" | custom-call | tf_op jit(solution)/shard_map/pallas_call | solution.py:779

commit v9 on v8

--- a/solution.py
+++ b/solution.py
@@ -410,25 +410,36 @@
 
     backward = {}
 
+    def send_bulk(off, comps, sem):
+        to = lax.rem(mi + off, n_modes)
+        rows = pl.ds(0, MID)
+        copy = pltpu.make_async_remote_copy(
+            src_ref=sendb.at[off, comps, rows],
+            dst_ref=back.at[mi, comps, rows],
+            send_sem=bwd_send.at[sem],
+            recv_sem=bwd_recv.at[sem],
+            device_id=(to, e),
+            device_id_type=MESH,
+        )
+        copy.start()
+        backward[sem] = copy
+
     def return_bulk(off):
         to = lax.rem(mi + off, n_modes)
-        result = coefficients(push_hi, push_lo, to)
-        for s in range(3):
-            force = result[s * BULK : (s + 1) * BULK] + LAMBDA_COEF * recv[to, s, FACE : FACE + BULK, :]
-            if off == 0:
-                back[mi, s] = force
-            else:
-                sendb[off, s] = force
-        if off:
-            backward[off] = pltpu.make_async_remote_copy(
-                src_ref=sendb.at[off, :, pl.ds(0, MID)],
-                dst_ref=back.at[mi, :, pl.ds(0, MID)],
-                send_sem=bwd_send.at[off],
-                recv_sem=bwd_recv.at[off],
-                device_id=(to, e),
-                device_id_type=MESH,
-            )
-            backward[off].start()
+        count = 1 if off == 2 else 3
+        for first in range(0, 3, count):
+            part = pl.ds(first * BULK, count * BULK)
+            result = coefficients(push_hi.at[part], push_lo.at[part], to)
+            for s in range(first, first + count):
+                held = recv[to, s, FACE : FACE + BULK, :]
+                at = (s - first) * BULK
+                force = result[at : at + BULK] + LAMBDA_COEF * held
+                if off == 0:
+                    back[mi, s] = force
+                else:
+                    sendb[off, s] = force
+            if off:
+                send_bulk(off, pl.ds(first, count), 2 * first if off == 2 else off)
 
     local[8].wait()
     return_bulk(2)
@@ -490,8 +501,8 @@
             copy.start()
             side_returns.append(copy)
     local[9].wait()
-    for off in (1, 3, 2):
-        backward[off].wait_recv()
+    for sem in (1, 3, 0, 2, 4):
+        backward[sem].wait_recv()
     for copy in side_returns:
         copy.wait_recv()
 
@@ -750,8 +761,8 @@
             dma((10,)),
             dma((ER, 3)),
             dma((ER, 3)),
-            dma((ER,)),
-            dma((ER,)),
+            dma((5,)),
+            dma((5,)),
             dma((2, 2)),
             dma((ER,)),
             dma((ER,)),

time: 45.8 us -> 46.3 us (1.011)
  Pallas kernels: 45.7 us -> 46.2 us
    pallas_call x1, Pallas kernels: 44.6 us -> 45.1 us  [on_device(): pl.pallas_call(functools.partial(kernel, grid_shape), out_shape=(vmem((3,...]
where the time goes in v9:
time: 46.3 us; the launch traced here: 46.2 us
  Pallas kernels  46.2 us (100%)
    pallas_call x1, Pallas kernels, on_device(): pl.pallas_call(functools.partial(kernel, grid_shape), out_shape=(vmem((3,...  45.1 us
    pallas_call x1, Pallas kernels, on_device(): pl.pallas_call(combine, out_shape=jax.ShapeDtypeStruct((3 * NODES * ER, L...  1.13 us

profile of v9, /device:TPU:1, one launch (start us, length us, event | category | flops | bytes accessed | tf_op | source)
XLA Modules:
  0.0 46.2 jit_solution(4823654415333347919)
XLA Ops:
  0.0 45.1 %shard_map.82 = (f32[3,3,400,128]{3,2,1,0:T(8,128)S(1)}, f32[9,128]{1,0:T(8,128)S(1)}) custom-call(s32[1,4]{1,0:T(1,128)} %slot_hbm.1, s32[1,64]{1,0:T(1,128)} %bitcast.8, f32[1200,128]{1,0:T(8,128)} %bitcast.7, bf16[224,384]{1,0:T(8,128)(2,1)} %constant.10.clone.slopes_hbm, bf16[4,112,384]{2,1,0:T(8,128)(2,1)} %constant.11.clone.stiff_hbm, ...), custom_call_target="tpu_custom_call" | custom-call | tf_op jit(solution)/shard_map/pallas_call | solution.py:724
  45.1 1.1 %shard_map.83 = f32[1200,128]{1,0:T(8,128)} custom-call(f32[3,3,400,128]{3,2,1,0:T(8,128)S(1)} %get-tuple-element.7.ordered, f32[9,128]{1,0:T(8,128)S(1)} %get-tuple-element.8.total_ref), custom_call_target="tpu_custom_call" | custom-call | tf_op jit(solution)/shard_map/pallas_call | solution.py:790
